TPU v7x, 256 devices: a whole 4x4x8 slice. The times are simulated.
256 devices in a mesh: seq: 64 (over z, x, core), head: 4 (over y).
Axes of the slice: x: 4, y: 4, z: 8, core: 2. Of those that a mesh axis runs over, the one named last changes fastest.
Arguments:
- queries: bfloat16 [16384, 2048], P('seq', 'head'), may hold values from -30 to 30
- key_rows: bfloat16 [16384, 2048], P('seq', 'head'), may hold values from -5 to 5
- value_rows: bfloat16 [16384, 2048], P('seq', 'head'), may hold values from -6 to 6
- out_grad: bfloat16 [16384, 2048], P('seq', 'head'), may hold values from -6 to 6
- random_blocks: int32 [4, 256, 3], P('head'), may hold values from 0 to 255, as said below
- global_blocks: int32 [2], replicated, may hold values from 0 to 255, as said below
Outputs:
- attended: bfloat16 [16384, 2048], P('seq', 'head')
- query_grad: bfloat16 [16384, 2048], P('seq', 'head')
- key_grad: bfloat16 [16384, 2048], P('seq', 'head')
- value_grad: bfloat16 [16384, 2048], P('seq', 'head')
Inputs may be any that keep to these rules, and one draw needn't show every extreme that they name: `random_blocks`: in each head group, the query blocks s * 4 to s * 4 + 3 of one segment name at most 1 random entries inside any one segment of 4 key blocks, and for every such query segment some key segment is named exactly 1 times. `global_blocks`: the global blocks are different from each other, and one of them is the last block, 255.
All inputs are finite; a program needn't handle non-finite values.
Results may differ from a plain program's by a relative error of at most 0.039.
Values may be sent and summed in bfloat16 or wider, within the bound.
A program may use at most 128 MiB of HBM per device.

v0:
```python
import math

import jax
import jax.numpy as jnp
from jax import lax
from jax.sharding import PartitionSpec as P

HEAD_DIM = 128
BLK = 64
GLOBALS = 2
RANDOMS = 3


def with_halo(block, sides, width):
    for axis, dim in sides:
        count = lax.axis_size(axis)
        forward = [(i, i + 1) for i in range(count - 1)]
        backward = [(target, source) for source, target in forward]
        low = lax.ppermute(
            lax.slice_in_dim(block, block.shape[dim] - width, None, axis=dim), axis, forward
        )
        high = lax.ppermute(lax.slice_in_dim(block, 0, width, axis=dim), axis, backward)
        block = jnp.concatenate([low, block, high], axis=dim)
    return block


def spread(value, axis, source):
    kept = jnp.where(lax.axis_index(axis) == source, value, 0).astype(value.dtype)
    return lax.psum(kept, axis)


def attend_group(inputs):
    query_rows, grad_rows, key_block, value_block, key_valid = inputs
    score_scale = 1.0 / math.sqrt(query_rows.shape[-1])
    scores = (
        jnp.einsum("nqhd,nkhd->nhqk", query_rows, key_block, preferred_element_type=jnp.float32)
        * score_scale
    )
    scores = jnp.where(key_valid[:, None, None, :], scores, -jnp.inf)
    row_max = jnp.max(scores, axis=3, keepdims=True)
    raw = jnp.exp(scores - row_max)
    total = jnp.sum(raw, axis=3, keepdims=True)
    weights = raw / total
    weights_b = weights.astype(jnp.bfloat16)
    attended = jnp.einsum(
        "nhqk,nkhd->nqhd", weights_b, value_block, preferred_element_type=jnp.float32
    ).astype(jnp.bfloat16)
    row_dot = jnp.sum(grad_rows.astype(jnp.float32) * attended.astype(jnp.float32), axis=-1)
    row_dot_t = jnp.transpose(row_dot, (0, 2, 1))
    weight_grads = jnp.einsum(
        "nqhd,nkhd->nhqk", grad_rows, value_block, preferred_element_type=jnp.float32
    )
    score_grads = (weights * (weight_grads - row_dot_t[:, :, :, None]) * score_scale).astype(
        jnp.bfloat16
    )
    query_grad = jnp.einsum(
        "nhqk,nkhd->nqhd", score_grads, key_block, preferred_element_type=jnp.float32
    ).astype(jnp.bfloat16)
    key_terms = jnp.einsum(
        "nhqk,nqhd->nkhd", score_grads, query_rows, preferred_element_type=jnp.float32
    ).astype(jnp.bfloat16)
    value_terms = jnp.einsum(
        "nhqk,nqhd->nkhd", weights_b, grad_rows, preferred_element_type=jnp.float32
    ).astype(jnp.bfloat16)
    row_stats = jnp.stack([row_max[..., 0], total[..., 0], row_dot_t], axis=1)
    return (attended, query_grad, key_terms, value_terms, row_stats)


def per_device(queries, key_rows, value_rows, out_grad, random_blocks, global_blocks):
    row_count, features = queries.shape
    segment = lax.axis_index("seq")
    segments = lax.axis_size("seq")
    head_count = features // HEAD_DIM
    block_count = row_count // BLK
    request_count = block_count * RANDOMS
    capacity = (request_count + segments - 1) // segments
    entries = 3 + GLOBALS + RANDOMS
    block_ids = jnp.arange(block_count, dtype=jnp.int32)
    key_value = jnp.stack([key_rows, value_rows])
    own_blocks = key_value.reshape(2, block_count, BLK, features)
    extended = with_halo(key_value, (("seq", 1),), BLK)
    ext_blocks = extended.reshape(2, block_count + 2, BLK, features)
    window = jnp.stack(
        [
            ext_blocks[:, 0:block_count],
            ext_blocks[:, 1 : block_count + 1],
            ext_blocks[:, 2 : block_count + 2],
        ],
        axis=2,
    )
    owner_of = global_blocks // block_count
    local_of = global_blocks % block_count
    fetched = []
    for number in range(GLOBALS):
        piece = lax.dynamic_index_in_dim(own_blocks, local_of[number], 1, keepdims=False)
        fetched.append(spread(piece, "seq", owner_of[number]))
    global_kv = jnp.stack(fetched, axis=1)
    all_lists = random_blocks[0].reshape(segments, request_count)
    my_list = lax.dynamic_index_in_dim(all_lists, segment, 0, keepdims=False)
    peer_ids = jnp.arange(segments, dtype=jnp.int32)
    my_owner = my_list // block_count
    owner_hits = (my_owner[:, None] == peer_ids[None, :]).astype(jnp.int32)
    my_slot = jnp.sum((jnp.cumsum(owner_hits, axis=0) - owner_hits) * owner_hits, axis=1)
    my_position = my_owner * capacity + my_slot
    wanted = (all_lists // block_count == segment).astype(jnp.int32)
    earlier = jnp.cumsum(wanted, axis=1) - wanted
    slot_ids = jnp.arange(capacity, dtype=jnp.int32)
    matches = wanted[:, :, None] * (earlier[:, :, None] == slot_ids[None, None, :]).astype(
        jnp.int32
    )
    requested = jnp.sum(matches * (all_lists % block_count + 1)[:, :, None], axis=1) - 1
    requested_flat = requested.reshape(segments * capacity)
    position_ids = jnp.arange(segments * capacity, dtype=jnp.int32)
    request_ids = jnp.arange(request_count, dtype=jnp.int32)
    source = jnp.sum(
        (my_position[:, None] == position_ids[None, :]).astype(jnp.int32) * request_ids[:, None],
        axis=0,
    )
    held_kv = jnp.take(own_blocks, jnp.maximum(requested_flat, 0), axis=1)
    outgoing = held_kv.reshape(2, segments, capacity, BLK, features)
    incoming = lax.all_to_all(outgoing, "seq", split_axis=1, concat_axis=1, tiled=True)
    random_kv = jnp.take(
        incoming.reshape(2, segments * capacity, BLK, features), my_position, axis=1
    )
    random_kv = random_kv.reshape(2, block_count, RANDOMS, BLK, features)
    global_rep = jnp.broadcast_to(global_kv[:, None], (2, block_count, GLOBALS, BLK, features))
    keys_all = jnp.concatenate([window, global_rep, random_kv], axis=2)
    left_ok = (block_ids > 0) | (segment > 0)
    right_ok = (block_ids < block_count - 1) | (segment < segments - 1)
    always_ok = jnp.broadcast_to((block_ids >= 0)[:, None], (block_count, GLOBALS + RANDOMS))
    entry_ok = jnp.concatenate(
        [left_ok[:, None], (block_ids >= 0)[:, None], right_ok[:, None], always_ok], axis=1
    )
    key_valid = jnp.repeat(entry_ok, BLK, axis=1)
    group_size = min(8, block_count)
    group_count = block_count // group_size
    query_shape = (group_count, group_size, BLK, head_count, HEAD_DIM)
    key_shape = (group_count, group_size, entries * BLK, head_count, HEAD_DIM)
    attended, query_grad, key_terms, value_terms, row_stats = lax.map(
        attend_group,
        (
            queries.reshape(query_shape),
            out_grad.reshape(query_shape),
            keys_all[0].reshape(key_shape),
            keys_all[1].reshape(key_shape),
            key_valid.reshape(group_count, group_size, entries * BLK),
        ),
    )
    grad_terms = jnp.stack([key_terms, value_terms]).reshape(2, block_count, entries, BLK, features)
    zero_block = jnp.zeros((2, 1, BLK, features), jnp.float32)
    gradient = grad_terms[:, :, 1].astype(jnp.float32)
    gradient = gradient + jnp.concatenate(
        [grad_terms[:, 1:, 0].astype(jnp.float32), zero_block], axis=1
    )
    gradient = gradient + jnp.concatenate(
        [zero_block, grad_terms[:, :-1, 2].astype(jnp.float32)], axis=1
    )
    rim_terms = jnp.concatenate([grad_terms[:, 0, 0], grad_terms[:, block_count - 1, 2]], axis=1)
    rim_back = with_halo(rim_terms, (("seq", 1),), BLK)
    gradient = gradient.at[:, 0].add(rim_back[:, :BLK].astype(jnp.float32))
    gradient = gradient.at[:, block_count - 1].add(rim_back[:, 3 * BLK :].astype(jnp.float32))
    global_terms = jnp.sum(grad_terms[:, :, 3 : 3 + GLOBALS].astype(jnp.float32), axis=1)
    global_total = lax.psum(global_terms, "seq")
    global_home = (global_blocks[:, None] == segment * block_count + block_ids[None, :]).astype(
        jnp.float32
    )
    gradient = gradient + jnp.einsum(
        "gb,xgkf->xbkf", global_home, global_total, precision=lax.Precision.HIGHEST
    )
    random_terms = grad_terms[:, :, 3 + GLOBALS :].reshape(2, request_count, BLK, features)
    returning = jnp.take(random_terms, source, axis=1).reshape(2, segments, capacity, BLK, features)
    arrived = lax.all_to_all(returning, "seq", split_axis=1, concat_axis=1, tiled=True).reshape(
        2, segments * capacity, BLK, features
    )
    landing = (requested_flat[:, None] == block_ids[None, :]).astype(jnp.bfloat16)
    gradient = gradient + jnp.einsum(
        "sb,xskf->xbkf", landing, arrived, preferred_element_type=jnp.float32
    )
    return (
        attended.reshape(row_count, features),
        query_grad.reshape(row_count, features),
        gradient[0].reshape(row_count, features).astype(jnp.bfloat16),
        gradient[1].reshape(row_count, features).astype(jnp.bfloat16),
    )


def solution(mesh):
    in_specs = (
        P("seq", "head"),
        P("seq", "head"),
        P("seq", "head"),
        P("seq", "head"),
        P("head", None, None),
        P(),
    )
    out_specs = (P("seq", "head"), P("seq", "head"), P("seq", "head"), P("seq", "head"))
    return jax.shard_map(
        per_device, mesh=mesh, in_specs=in_specs, out_specs=out_specs, check_vma=False
    )
```

profile of v0, /device:TPU:1, one launch (start us, length us, event | category | flops | bytes accessed | tf_op | source)
XLA Modules:
  0.0 603.5 jit_solution(4000040666656287219)
XLA Ops:
  7.2 0.8 copy.99
  8.0 0.7 broadcast_compare_fusion
  9.3 0.2 fusion.55
  9.9 0.2 select_reduce_fusion.1
  10.2 1.1 pad_maximum_fusion.2
  11.3 5.3 gather_fusion
  16.6 7.5 %fusion.2 = bf16[2,64,1,64,512]{4,3,0,2,1:T(8,128)(2,1)} fusion(bf16[64,2,64,512]{3,2,1,0:T(8,128)(2,1)} %gather_fusion, pred[64]{0:T(512)(128)(4,1)S(1)} %get-tuple-element.85), kind=kLoop, calls=%fused_computation.7 | loop fusion | flops 4194304 | bytes 16777280 | tf_op jit(solution)/shard_map/jit(_take)/select_n | solution.py:119
  24.1 13.3 %all-to-all-start = ((bf16[2,64,1,64,512]{4,3,0,2,1:T(8,128)(2,1)}), bf16[2,64,1,64,512]{4,3,0,2,1:T(8,128)(2,1)}, u32[]{:S(2)}, u32[]{:S(2)}) async-start(bf16[2,64,1,64,512]{4,3,0,2,1:T(8,128)(2,1)} %fusion.2), calls=%async_computation | async-start | bytes 16777216 | tf_op jit(solution)/shard_map/all_to_all | solution.py:121
  37.5 2.6 collective-permute-start.1
  40.1 3.1 collective-permute-start
  43.2 0.6 fusion.90
  49.0 0.7 fusion.59
  50.6 225.5 %all-reduce.8.cloned.1.call-done = (bf16[2,1,64,512]{3,2,1,0:T(8,128)(2,1)}, bf16[2,1,64,512]{3,2,1,0:T(8,128)(2,1)}) async-done(((bf16[2,1,64,512]{3,2,1,0:T(8,128)(2,1)}, bf16[2,1,64,512]{3,2,1,0:T(8,128)(2,1)}), (bf16[2,1,64,512]{3,2,1,0:T(8,128)(2,1)}, bf16[2,1,64,512]{3,2,1,0:T(8,128)(2,1)})) %all-reduce.8.cloned.1.call-update) | async-done | bytes 262160 | tf_op jit(solution)/shard_map/psum | solution.py:29
  276.1 1.0 pad_maximum_fusion.3
  277.2 0.8 fusion.47
  278.0 0.8 fusion.46
  278.8 0.8 fusion.45
  279.7 1.1 broadcast_dynamic-update-slice_fusion
  280.8 7.7 %copy.200 = bf16[2,64,1,64,512]{4,3,1,0,2:T(8,128)(2,1)} copy(bf16[2,64,1,64,512]{4,3,0,2,1:T(8,128)(2,1)} %all-to-all-done) | data formatting | bytes 16777216 | tf_op jit(solution)/shard_map/all_to_all | solution.py:121
  288.5 4.0 gather_fusion.1
  292.6 1.7 select_dynamic-update-slice_fusion
  294.3 4.0 fusion.88
  298.3 2.0 squeeze.60
  300.3 2.5 squeeze.61
  302.9 0.8 fusion.18
  303.7 0.5 copy-done.2
  304.2 1.0 fusion.92
  305.3 1.0 convert_bitcast_fusion
  306.3 0.6 copy-done.5
  306.8 1.5 multiply_reduce_fusion
  308.3 1.9 fusion.7
  310.2 3.0 copy.125
  313.2 2.7 stack.55
  315.9 0.8 convert_bitcast_fusion.1
  316.7 3.0 copy.123
  319.7 4.1 stack.54
  323.8 1.3 pad_maximum_fusion
  325.0 1.3 copy.134
  326.3 6.7 %gather_fusion.2 = bf16[64,2,64,512]{3,2,1,0:T(8,128)(2,1)} fusion(bf16[2,12,64,512]{3,2,1,0:T(8,128)(2,1)} %copy.134, s32[1024]{0:T(1024)S(1)} %get-tuple-element.88), kind=kCustom, calls=%fused_computation.2 | custom fusion | bytes 16777472 | tf_op jit(solution)/shard_map/jit(_take)/gather | solution.py:171
  333.0 7.5 %fusion.1 = bf16[2,64,1,64,512]{4,3,0,2,1:T(8,128)(2,1)} fusion(bf16[64,2,64,512]{3,2,1,0:T(8,128)(2,1)} %gather_fusion.2, pred[64]{0:T(512)(128)(4,1)S(1)} %get-tuple-element.84), kind=kLoop, calls=%fused_computation.5 | loop fusion | flops 4194304 | bytes 16777280 | tf_op jit(solution)/shard_map/jit(_take)/select_n | solution.py:171
  340.5 6.9 %all-to-all-start.1 = ((bf16[2,64,1,64,512]{4,3,0,2,1:T(8,128)(2,1)}), bf16[2,64,1,64,512]{4,3,0,2,1:T(8,128)(2,1)}, u32[]{:S(2)}, u32[]{:S(2)}) async-start(bf16[2,64,1,64,512]{4,3,0,2,1:T(8,128)(2,1)} %fusion.1), calls=%async_computation.1 | async-start | bytes 16777216 | tf_op jit(solution)/shard_map/all_to_all | solution.py:172
  347.3 0.3 all-reduce.6.cloned.1.call-start
  347.6 1.2 copy.116
  348.8 0.7 copy.202
  349.5 2.2 fusion.37
  351.7 0.2 copy.121
  351.9 0.7 copy.201
  352.7 3.5 collective-permute-start.2
  356.2 1.9 collective-permute-start.3
  358.3 1.2 copy.133
  359.6 1.2 maximum_bitcast_fusion.2
  360.8 0.5 copy-done.1
  361.3 0.2 fusion.40
  361.5 8.6 %collective-permute-done.2 = bf16[2,64,512]{2,1,0:T(8,128)(2,1)S(1)} collective-permute-done((bf16[2,64,512]{2,1,0:T(8,128)(2,1)S(1)}, bf16[2,64,512]{2,1,0:T(8,128)(2,1)S(1)}, u32[]{:S(2)}, u32[]{:S(2)}) %collective-permute-start.2) | collective-permute-done | bytes 131104 | tf_op jit(solution)/shard_map/ppermute | solution.py:19
  370.2 0.7 copy.132
  370.9 8.7 %collective-permute-done.3 = bf16[2,64,512]{2,1,0:T(8,128)(2,1)S(1)} collective-permute-done((bf16[2,64,512]{2,1,0:T(8,128)(2,1)S(1)}, bf16[2,64,512]{2,1,0:T(8,128)(2,1)S(1)}, u32[]{:S(2)}, u32[]{:S(2)}) %collective-permute-start.3) | collective-permute-done | bytes 131104 | tf_op jit(solution)/shard_map/ppermute | solution.py:22
  379.7 0.3 copy_add_fusion
  380.0 2.5 scatter-add.9
  382.6 152.1 %all-to-all-done.1 = bf16[2,64,1,64,512]{4,3,0,2,1:T(8,128)(2,1)} async-done(((bf16[2,64,1,64,512]{4,3,0,2,1:T(8,128)(2,1)}), bf16[2,64,1,64,512]{4,3,0,2,1:T(8,128)(2,1)}, u32[]{:S(2)}, u32[]{:S(2)}) %all-to-all-start.1) | async-done | bytes 8388640 | tf_op jit(solution)/shard_map/all_to_all | solution.py:172
  534.6 8.0 %fusion.22 = f32[2,4,64,512]{3,1,2,0:T(4,128)S(1)} fusion(bf16[2,64,1,64,512]{4,3,0,2,1:T(8,128)(2,1)} %all-to-all-done.1, s32[64]{0:T(128)S(1)} %get-tuple-element.72), kind=kOutput, calls=%fused_computation.33 | convolution fusion | flops 33554688 | bytes 9437440 | tf_op jit(solution)/shard_map/sb,xskf->xbkf/dot_general | solution.py:176
  542.6 49.9 %all-reduce.6.cloned.1.call-done = f32[2,2,64,512]{3,1,2,0:T(2,128)} async-done(((f32[2,2,64,512]{3,1,2,0:T(2,128)}), f32[2,2,64,512]{3,1,2,0:T(2,128)}) %all-reduce.6.cloned.1.call-update) | async-done | bytes 524304 | tf_op jit(solution)/shard_map/psum | solution.py:163
  592.5 2.5 fusion.27
  595.1 0.7 copy.137
  595.9 0.7 copy.138
  (65 shorter events, 2.6 us)
Async XLA Ops:
  24.1 13.4 %copy-start.3 = (bf16[256,512]{1,0:T(8,128)(2,1)S(1)}, bf16[256,512]{1,0:T(8,128)(2,1)}, u32[]{:S(2)}) copy-start(bf16[256,512]{1,0:T(8,128)(2,1)} %param.12) | copy-start | bytes 786436
  24.1 13.4 %copy-start.4 = (bf16[256,512]{1,0:T(8,128)(2,1)S(1)}, bf16[256,512]{1,0:T(8,128)(2,1)}, u32[]{:S(2)}) copy-start(bf16[256,512]{1,0:T(8,128)(2,1)} %param.11) | copy-start | bytes 786436
  24.1 19.1 %copy-start.9 = (s32[2]{0:T(128)S(1)}, s32[2]{0:T(128)}, u32[]{:S(2)}) copy-start(s32[2]{0:T(128)} %param.15) | copy-start | bytes 28
  24.1 256.7 %all-to-all-start = ((bf16[2,64,1,64,512]{4,3,0,2,1:T(8,128)(2,1)}), bf16[2,64,1,64,512]{4,3,0,2,1:T(8,128)(2,1)}, u32[]{:S(2)}, u32[]{:S(2)}) async-start(bf16[2,64,1,64,512]{4,3,0,2,1:T(8,128)(2,1)} %fusion.2), calls=%async_computation | async-start | bytes 16777216 | tf_op jit(solution)/shard_map/all_to_all | solution.py:121
  37.4 12.9 %copy-start.6 = (bf16[256,512]{1,0:T(8,128)(2,1)S(1)}, bf16[256,512]{1,0:T(8,128)(2,1)}, u32[]{:S(2)}) copy-start(bf16[256,512]{1,0:T(8,128)(2,1)} %param.13) | copy-start | bytes 786436
  37.4 13.0 %copy-start.7 = (bf16[256,512]{1,0:T(8,128)(2,1)S(1)}, bf16[256,512]{1,0:T(8,128)(2,1)}, u32[]{:S(2)}) copy-start(bf16[256,512]{1,0:T(8,128)(2,1)} %param.10) | copy-start | bytes 786436
  37.4 238.7 %all-reduce.8.cloned.1.call-start = ((), (), s32[]{:S(2)}) async-start(), calls=%async_computation.3 | async-start | bytes 524288 | tf_op jit(solution)/shard_map/psum | solution.py:29
  37.5 239.6 %collective-permute-start.1 = (bf16[2,64,512]{2,1,0:T(8,128)(2,1)S(1)}, bf16[2,64,512]{2,1,0:T(8,128)(2,1)S(1)}, u32[]{:S(2)}, u32[]{:S(2)}) collective-permute-start(bf16[2,64,512]{2,1,0:T(8,128)(2,1)S(1)} %get-tuple-element.71), channel_id=1, source_target_pairs={{4,0},{8,4},{12,8},{16,12},{20,16},{24,20},{28,24},{32,28},{36,32}... | collective-permute-start | bytes 393224 | tf_op jit(solution)/shard_map/ppermute | solution.py:22
  40.1 237.0 %collective-permute-start = (bf16[2,64,512]{2,1,0:T(8,128)(2,1)S(1)}, bf16[2,64,512]{2,1,0:T(8,128)(2,1)S(1)}, u32[]{:S(2)}, u32[]{:S(2)}) collective-permute-start(bf16[2,64,512]{2,1,0:T(8,128)(2,1)S(1)} %get-tuple-element.70), channel_id=1, source_target_pairs={{0,4},{4,8},{8,12},{12,16},{16,20},{20,24},{24,28},{28,32},{32,36}... | collective-permute-start | bytes 393224 | tf_op jit(solution)/shard_map/ppermute | solution.py:19
  50.4 255.9 %copy-start.8 = (bf16[4,64,4,128]{3,2,1,0:T(4,128)(2,1)}, bf16[4,64,4,128]{3,2,1,0:T(4,128)(2,1)S(1)}, u32[]{:S(2)}) copy-start(bf16[4,64,4,128]{3,2,1,0:T(4,128)(2,1)S(1)} %squeeze.63) | copy-start | bytes 786436
  302.9 1.3 copy-start.2
  305.2 1.6 copy-start.5
  340.5 194.1 %all-to-all-start.1 = ((bf16[2,64,1,64,512]{4,3,0,2,1:T(8,128)(2,1)}), bf16[2,64,1,64,512]{4,3,0,2,1:T(8,128)(2,1)}, u32[]{:S(2)}, u32[]{:S(2)}) async-start(bf16[2,64,1,64,512]{4,3,0,2,1:T(8,128)(2,1)} %fusion.1), calls=%async_computation.1 | async-start | bytes 16777216 | tf_op jit(solution)/shard_map/all_to_all | solution.py:172
  347.3 245.1 %all-reduce.6.cloned.1.call-start = ((), (), s32[]{:S(2)}) async-start(), calls=%async_computation.2 | async-start | bytes 1048576 | tf_op jit(solution)/shard_map/psum | solution.py:163
  349.5 3.1 copy-start
  352.7 17.5 %collective-permute-start.2 = (bf16[2,64,512]{2,1,0:T(8,128)(2,1)S(1)}, bf16[2,64,512]{2,1,0:T(8,128)(2,1)S(1)}, u32[]{:S(2)}, u32[]{:S(2)}) collective-permute-start(bf16[2,64,512]{2,1,0:T(8,128)(2,1)S(1)} %get-tuple-element.61), channel_id=1, source_target_pairs={{0,4},{4,8},{8,12},{12,16},{16,20},{20,24},{24,28},{28,32},{32,36}... | collective-permute-start | bytes 393224 | tf_op jit(solution)/shard_map/ppermute | solution.py:19
  356.2 23.4 %collective-permute-start.3 = (bf16[2,64,512]{2,1,0:T(8,128)(2,1)S(1)}, bf16[2,64,512]{2,1,0:T(8,128)(2,1)S(1)}, u32[]{:S(2)}, u32[]{:S(2)}) collective-permute-start(bf16[2,64,512]{2,1,0:T(8,128)(2,1)S(1)} %get-tuple-element.60), channel_id=1, source_target_pairs={{4,0},{8,4},{12,8},{16,12},{20,16},{24,20},{28,24},{32,28},{36,32}... | collective-permute-start | bytes 393224 | tf_op jit(solution)/shard_map/ppermute | solution.py:22
  359.6 1.8 copy-start.1
Sparse Core Ops, SparseCore 0:
  49.9 226.1 all-reduce.7
  359.7 232.7 all-reduce.5
where the time goes:
time: 606 us; the launch traced here: 603 us
  waiting for transfers between devices  445 us (73%)
  local copies, waits for them, and re-layouts  63.2 us (10%)
  starting transfers between devices  31.6 us (5%)
  other arithmetic  25.6 us (4%)
  between operations  19.7 us (3%)
  matrix products  18.5 us (3%)
    psum x1, waiting for transfers between devices, spread(): return lax.psum(kept, axis)  225 us
    all_to_all x1, waiting for transfers between devices, per_device(): lax.all_to_all(returning, 'seq', split_axis=1, concat_axis=1, tiled=True)  152 us
    psum x1, waiting for transfers between devices, per_device(): global_total = lax.psum(global_terms, 'seq')  49.9 us
    all_to_all x1, starting transfers between devices, per_device(): lax.all_to_all(outgoing, 'seq', split_axis=1, concat_axis=1, tiled=True)  13.3 us
  transfers between devices with their start and end apart: 8, of which 5 were waited for; matrix products, arithmetic and copies ran while one was open for 4% of the time, Pallas kernels for 0%

commit v1 on v0

v1 whole, which is shorter than its diff:
```python
import functools
import math

import jax
import jax.numpy as jnp
from jax import lax
from jax.experimental import pallas as pl
from jax.experimental.pallas import tpu as pltpu
from jax.sharding import PartitionSpec as P

HEAD_DIM = 128
BLK = 64
NZ = 8
NX = 4
NC = 2
NSEQ = NZ * NX * NC
BLK_DEV = 4
REQ = 12
SLOTS = 2 * REQ + 2
VMEM_LIMIT = 56 * 1024 * 1024


def seq_of(z, x, c):
    return (lax.rem(z + NZ, NZ) * NX + lax.rem(x + NX, NX)) * NC + c


def place():
    me = lax.axis_index("seq")
    z = me // (NX * NC)
    x = lax.rem(me // NC, NX)
    c = lax.rem(me, NC)
    return me, z, x, c


def remote(src, dst, send_sem, recv_sem, target):
    return pltpu.make_async_remote_copy(
        src_ref=src,
        dst_ref=dst,
        send_sem=send_sem,
        recv_sem=recv_sem,
        device_id={"seq": target},
        device_id_type=pl.DeviceIdType.MESH,
    )


def greet(partners):
    barrier = pltpu.get_barrier_semaphore()
    for partner in partners:
        pl.semaphore_signal(
            barrier, inc=1, device_id={"seq": partner}, device_id_type=pl.DeviceIdType.MESH
        )
    pl.semaphore_wait(barrier, len(partners))


def gather_kernel(
    table, globals_, k_ref, v_ref, out_ref, halo_ref,
    ag, s1_out, s1_in, s2_out, s2_in, s3_out, s3_in, give,
    pair_sem, halo_send, halo_recv, z_send, z_recv, x_send, x_recv, give_sem,
):
    me, z, x, c = place()
    other = 1 - c
    sibling = seq_of(z, x, other)
    after = lax.rem(me + 1, NSEQ)
    before = lax.rem(me + NSEQ - 1, NSEQ)
    sigma = 1 - 2 * c
    far = seq_of(z, x + sigma, c)
    near = seq_of(z, x - sigma, c)
    zs = (seq_of(z + 1, x, c), seq_of(z - 1, x, c))
    greet((after, before, zs[0], zs[1], far, near))

    def pair_copy(src):
        return remote(
            src, ag.at[pl.ds(z * 8 + c * 4, 4)], pair_sem.at[0], pair_sem.at[1], sibling
        )

    own = ag.at[pl.ds(z * 8 + c * 4, 4)]

    @pl.when(c == 0)
    def _():
        pair_copy(v_ref).start()
        own[...] = k_ref[...]

    @pl.when(c == 1)
    def _():
        pair_copy(k_ref).start()
        own[...] = v_ref[...]

    def z_piece(direction, step, half):
        origin = lax.rem(z + NZ - (step - 1), NZ) if direction == 0 else lax.rem(z + step - 1, NZ)
        piece = ag.at[pl.ds(origin * 8 + half * 4, 4)]
        return remote(
            piece,
            piece,
            z_send.at[direction, step - 1, half],
            z_recv.at[direction, step - 1, half],
            zs[direction],
        )

    for direction in range(2):
        z_piece(direction, 1, c).start()
    pair_copy(v_ref).wait()
    for direction in range(2):
        z_piece(direction, 1, other).start()

    halos = []
    for number, ref in enumerate((k_ref, v_ref)):
        halos.append(
            remote(
                ref.at[3], halo_ref.at[number, 0], halo_send.at[number, 0],
                halo_recv.at[number, 0], after,
            )
        )
        halos.append(
            remote(
                ref.at[0], halo_ref.at[number, 1], halo_send.at[number, 1],
                halo_recv.at[number, 1], before,
            )
        )
    for copy in halos:
        copy.start()

    last = {(0, 0): 4, (0, 1): 3, (1, 0): 3, (1, 1): 4}
    for step in range(1, 5):
        for half in range(2):
            for direction in range(2):
                if step <= last[direction, half]:
                    z_piece(direction, step, half).wait_recv()
                    if step + 1 <= last[direction, half]:
                        z_piece(direction, step + 1, half).start()

    def request(chip, slot):
        if slot < 2 * REQ:
            return table[seq_of(z, chip, 0) * REQ + slot]
        return globals_[slot - 2 * REQ]

    def wanted(chip, slot):
        block = request(chip, slot)
        source = lax.rem(lax.div(block, 8), NX)
        return source, ag[lax.div(block, 32) * 8 + lax.rem(block, 8)]

    def x_copy(number, src, dst, target):
        return remote(src, dst, x_send.at[number], x_recv.at[number], target)

    first = x_copy(0, s1_out, s1_in, far)
    for slot in range(SLOTS):
        s1_out[slot] = wanted(x + 2, slot)[1]
    first.start()
    third = x_copy(2, s3_out, s3_in, near)
    for slot in range(SLOTS):
        s3_out[slot] = wanted(x - sigma, slot)[1]
    third.start()
    first.wait_recv()
    second = x_copy(1, s2_out, s2_in, far)
    for slot in range(SLOTS):
        source, mine = wanted(x + sigma, slot)
        s2_out[slot] = jnp.where(source == x, mine, s1_in[slot])
    second.start()
    third.wait_recv()
    second.wait_recv()

    here = lax.rem(x + sigma + NX, NX)

    def chosen(slot_of_table, slot):
        block = slot_of_table
        source = lax.rem(lax.div(block, 8), NX)
        mine = ag[lax.div(block, 32) * 8 + lax.rem(block, 8)]
        return jnp.where(
            source == x, mine, jnp.where(source == here, s3_in[slot], s2_in[slot])
        )

    for i in range(REQ):
        slot = other * REQ + i
        give[i] = chosen(table[seq_of(z, x, 0) * REQ + slot], slot)
    for i in range(2):
        value = chosen(globals_[i], 2 * REQ + i)
        give[REQ + i] = value
        out_ref[c, REQ + i] = value
    handed = remote(give, out_ref.at[c], give_sem.at[0], give_sem.at[1], sibling)
    handed.start()
    for i in range(REQ):
        slot = c * REQ + i
        out_ref[c, i] = chosen(table[seq_of(z, x, 0) * REQ + slot], slot)

    for copy in halos:
        copy.wait()
    for step in range(1, 5):
        for half in range(2):
            for direction in range(2):
                if step <= last[direction, half]:
                    z_piece(direction, step, half).wait_send()
    first.wait_send()
    second.wait_send()
    third.wait_send()
    handed.wait()


def gather(table, globals_, k, v):
    features = k.shape[-1]
    big = pltpu.VMEM((SLOTS, BLK, features), jnp.bfloat16)
    vmem = pl.BlockSpec(memory_space=pltpu.VMEM)
    smem = pl.BlockSpec(memory_space=pltpu.SMEM)
    dma = pltpu.SemaphoreType.DMA
    return pl.pallas_call(
        gather_kernel,
        out_shape=(
            jax.ShapeDtypeStruct((2, REQ + 2, BLK, features), jnp.bfloat16),
            jax.ShapeDtypeStruct((2, 2, BLK, features), jnp.bfloat16),
        ),
        in_specs=[smem, smem, vmem, vmem],
        out_specs=(vmem, vmem),
        scratch_shapes=[
            pltpu.VMEM((NZ * 8, BLK, features), jnp.bfloat16),
            big, big, big, big, big, big,
            pltpu.VMEM((REQ + 2, BLK, features), jnp.bfloat16),
            dma((2,)), dma((2, 2)), dma((2, 2)), dma((2, 4, 2)), dma((2, 4, 2)),
            dma((3,)), dma((3,)), dma((2,)),
        ],
        compiler_params=pltpu.CompilerParams(
            collective_id=0, has_side_effects=True, vmem_limit_bytes=VMEM_LIMIT
        ),
        name="gather_blocks",
    )(table, globals_, k, v)


def nt(a, b):
    return lax.dot_general(a, b, (((1,), (1,)), ((), ())), preferred_element_type=jnp.float32)


def tn(a, b):
    return lax.dot_general(a, b, (((0,), (0,)), ((), ())), preferred_element_type=jnp.float32)


def nn(a, b):
    return lax.dot_general(a, b, (((1,), (0,)), ((), ())), preferred_element_type=jnp.float32)


def attend_kernel(
    q_ref, g_ref, k_ref, v_ref, halo_ref, slot_ref,
    att_ref, qg_ref, wacc_ref, term_ref, rim_ref, acc, gacc,
):
    me = lax.axis_index("seq")
    features = q_ref.shape[-1]
    heads = features // HEAD_DIM
    scale = 1.0 / math.sqrt(HEAD_DIM)
    lane_head = lax.broadcasted_iota(jnp.int32, (BLK, features), 1) // HEAD_DIM
    acc[...] = jnp.zeros_like(acc)
    gacc[...] = jnp.zeros_like(gacc)

    def spread(rows):
        zero = jnp.zeros_like(rows)
        return jnp.concatenate(
            [jnp.where(lane_head == h, rows, zero) for h in range(heads)], axis=0
        )

    def diagonal(full):
        return jnp.concatenate(
            [
                full[h * BLK : (h + 1) * BLK, h * HEAD_DIM : (h + 1) * HEAD_DIM]
                for h in range(heads)
            ],
            axis=1,
        )

    for b in range(BLK_DEV):
        def listed(number, own):
            window = [
                halo_ref[number, 0] if b == 0 else own[b - 1],
                own[b],
                halo_ref[number, 1] if b == BLK_DEV - 1 else own[b + 1],
            ]
            extra = [slot_ref[number, REQ], slot_ref[number, REQ + 1]]
            random = [slot_ref[number, 3 * b + i] for i in range(3)]
            return jnp.concatenate(window + extra + random, axis=0)

        keys = listed(0, k_ref)
        values = listed(1, v_ref)
        query = spread(q_ref[b])
        grad = spread(g_ref[b])
        scores = nt(keys, query) * scale
        if b == 0:
            scores = jnp.concatenate(
                [jnp.where(me == 0, -jnp.inf, scores[:BLK]), scores[BLK:]], axis=0
            )
        if b == BLK_DEV - 1:
            scores = jnp.concatenate(
                [
                    scores[: 2 * BLK],
                    jnp.where(me == NSEQ - 1, -jnp.inf, scores[2 * BLK : 3 * BLK]),
                    scores[3 * BLK :],
                ],
                axis=0,
            )
        row_max = jnp.max(scores, axis=0, keepdims=True)
        raw = jnp.exp(scores - row_max)
        weights = raw * (1.0 / jnp.sum(raw, axis=0, keepdims=True))
        weights_b = weights.astype(jnp.bfloat16)
        weight_grads = nt(values, grad)
        row_dot = jnp.sum(weights_b.astype(jnp.float32) * weight_grads, axis=0, keepdims=True)
        score_grads = (weights * (weight_grads - row_dot) * scale).astype(jnp.bfloat16)
        att_ref[b] = diagonal(tn(weights_b, values)).astype(jnp.bfloat16)
        qg_ref[b] = diagonal(tn(score_grads, keys)).astype(jnp.bfloat16)
        for number, terms in enumerate((nn(score_grads, query), nn(weights_b, grad))):
            for i in range(3):
                acc[number, b + i] += terms[i * BLK : (i + 1) * BLK]
            for i in range(2):
                gacc[number, i] += terms[(3 + i) * BLK : (4 + i) * BLK]
            for i in range(3):
                term_ref[number, 3 * b + i] = terms[(5 + i) * BLK : (6 + i) * BLK].astype(
                    jnp.bfloat16
                )
    for number in range(2):
        for i in range(2):
            term_ref[number, REQ + i] = gacc[number, i].astype(jnp.bfloat16)
        rim_ref[number, 0] = acc[number, 0].astype(jnp.bfloat16)
        rim_ref[number, 1] = acc[number, BLK_DEV + 1].astype(jnp.bfloat16)
        for i in range(BLK_DEV):
            wacc_ref[number, i] = acc[number, i + 1]


def attend(q, g, k, v, halo, slots):
    features = q.shape[-1]
    vmem = pl.BlockSpec(memory_space=pltpu.VMEM)
    own = jax.ShapeDtypeStruct((BLK_DEV, BLK, features), jnp.bfloat16)
    return pl.pallas_call(
        attend_kernel,
        out_shape=(
            own,
            own,
            jax.ShapeDtypeStruct((2, BLK_DEV, BLK, features), jnp.float32),
            jax.ShapeDtypeStruct((2, REQ + 2, BLK, features), jnp.bfloat16),
            jax.ShapeDtypeStruct((2, 2, BLK, features), jnp.bfloat16),
        ),
        in_specs=[vmem] * 6,
        out_specs=(vmem,) * 5,
        scratch_shapes=[
            pltpu.VMEM((2, BLK_DEV + 2, BLK, features), jnp.float32),
            pltpu.VMEM((2, 2, BLK, features), jnp.float32),
        ],
        compiler_params=pltpu.CompilerParams(vmem_limit_bytes=VMEM_LIMIT),
        name="attend_blocks",
    )(q, g, k, v, halo, slots)


def spread_kernel(
    term_ref, rim_ref, all_ref, edge_ref, theirs,
    pair_sem, rim_send, rim_recv, x_send, x_recv, g_send, g_recv,
):
    me, z, x, c = place()
    other = 1 - c
    sibling = seq_of(z, x, other)
    after = lax.rem(me + 1, NSEQ)
    before = lax.rem(me + NSEQ - 1, NSEQ)
    sigma = 1 - 2 * c
    xs = (seq_of(z, x + sigma, c), seq_of(z, x - sigma, c))
    greet((after, before, xs[0], xs[1]))
    pair = remote(term_ref.at[other], theirs, pair_sem.at[0], pair_sem.at[1], sibling)
    pair.start()

    def part(chip, core):
        return all_ref.at[lax.rem(chip + NX, NX), pl.ds(core * REQ, REQ)]

    def rest(chip):
        return all_ref.at[lax.rem(chip + NX, NX), pl.ds(2 * REQ, 2)]

    def send(number, ref, direction, core):
        return remote(
            ref, ref, x_send.at[number, core], x_recv.at[number, core], xs[direction]
        )

    for i in range(REQ):
        all_ref[x, c * REQ + i] = term_ref[c, i]
    for number in range(2):
        send(number, part(x, c), number, c).start()
    edges = []
    for number in range(2):
        edges.append(
            remote(
                rim_ref.at[number, 1], edge_ref.at[number, 0], rim_send.at[number, 0],
                rim_recv.at[number, 0], after,
            )
        )
        edges.append(
            remote(
                rim_ref.at[number, 0], edge_ref.at[number, 1], rim_send.at[number, 1],
                rim_recv.at[number, 1], before,
            )
        )
    pair.wait_recv()
    for i in range(REQ):
        all_ref[x, other * REQ + i] = theirs[i]
    for number in range(2):
        send(number, part(x, other), number, other).start()
    for i in range(2):
        total = term_ref[c, REQ + i].astype(jnp.float32) + theirs[REQ + i].astype(jnp.float32)
        all_ref[x, 2 * REQ + i] = total.astype(jnp.bfloat16)
    for number in range(2):
        remote(rest(x), rest(x), g_send.at[number], g_recv.at[number], xs[number]).start()
    for copy in edges:
        copy.start()
    for core in (c, other):
        send(0, part(x - sigma, core), 0, core).wait_recv()
        send(2, part(x - sigma, core), 0, core).start()
    remote(rest(x), rest(x - sigma), g_send.at[0], g_recv.at[0], xs[0]).wait_recv()
    remote(rest(x - sigma), rest(x - sigma), g_send.at[2], g_recv.at[2], xs[0]).start()
    for number in (1, 2):
        for core in (c, other):
            send(number, part(x, core), 0, core).wait_recv()
        remote(rest(x), rest(x), g_send.at[number], g_recv.at[number], xs[0]).wait_recv()
    for number in range(3):
        for core in (c, other):
            send(number, part(x, core), 0, core).wait_send()
        remote(rest(x), rest(x), g_send.at[number], g_recv.at[number], xs[0]).wait_send()
    pair.wait_send()
    for copy in edges:
        copy.wait()


def spread_terms(terms, rims):
    features = terms.shape[-1]
    vmem = pl.BlockSpec(memory_space=pltpu.VMEM)
    dma = pltpu.SemaphoreType.DMA
    return pl.pallas_call(
        spread_kernel,
        out_shape=(
            jax.ShapeDtypeStruct((NX, SLOTS, BLK, features), jnp.bfloat16),
            jax.ShapeDtypeStruct((2, 2, BLK, features), jnp.bfloat16),
        ),
        in_specs=[vmem, vmem],
        out_specs=(vmem, vmem),
        scratch_shapes=[
            pltpu.VMEM((REQ + 2, BLK, features), jnp.bfloat16),
            dma((2,)), dma((2, 2)), dma((2, 2)), dma((3, 2)), dma((3, 2)), dma((3,)), dma((3,)),
        ],
        compiler_params=pltpu.CompilerParams(
            collective_id=1, has_side_effects=True, vmem_limit_bytes=VMEM_LIMIT
        ),
        name="spread_terms",
    )(terms, rims)


def land_kernel(table, globals_, all_ref, acc_ref):
    me, z, x, c = place()
    acc_ref[...] = jnp.zeros_like(acc_ref)

    def add(chip, slot, block):
        @pl.when(lax.rem(lax.div(block, 8), NX) == x)
        def _():
            at = lax.div(block, 32) * 8 + lax.rem(block, 8)
            acc_ref[at] += all_ref[chip, slot].astype(jnp.float32)

    @pl.loop(0, NX)
    def _(chip):
        @pl.loop(0, 2 * REQ)
        def _(slot):
            add(chip, slot, table[seq_of(z, chip, 0) * REQ + slot])

        for i in range(2):
            add(chip, 2 * REQ + i, globals_[i])


def land(table, globals_, everything):
    features = everything.shape[-1]
    vmem = pl.BlockSpec(memory_space=pltpu.VMEM)
    smem = pl.BlockSpec(memory_space=pltpu.SMEM)
    return pl.pallas_call(
        land_kernel,
        out_shape=jax.ShapeDtypeStruct((NZ * 8, BLK, features), jnp.float32),
        in_specs=[smem, smem, vmem],
        out_specs=vmem,
        compiler_params=pltpu.CompilerParams(vmem_limit_bytes=VMEM_LIMIT),
        name="land_terms",
    )(table, globals_, everything)


def scatter_kernel(acc_ref, out_ref, send_buf, recv_buf, give, z_send, z_recv, give_sem):
    me, z, x, c = place()
    other = 1 - c
    sibling = seq_of(z, x, other)
    zs = (seq_of(z + 1, x, c), seq_of(z - 1, x, c))
    greet((sibling, zs[0], zs[1]))
    start = {(0, 0): 4, (0, 1): 3, (1, 0): 3, (1, 1): 4}

    def piece(direction, distance, half):
        return remote(
            send_buf.at[direction, distance - 1, half],
            recv_buf.at[direction, distance - 1, half],
            z_send.at[direction, distance - 1, half],
            z_recv.at[direction, distance - 1, half],
            zs[direction],
        )

    for distance in range(4, 0, -1):
        for half in range(2):
            for direction in range(2):
                if distance > start[direction, half]:
                    continue
                target = lax.rem(z + (distance if direction == 0 else NZ - distance), NZ)
                total = acc_ref[pl.ds(target * 8 + half * 4, 4)]
                if distance < start[direction, half]:
                    piece(direction, distance + 1, half).wait_recv()
                    total += recv_buf[direction, distance, half].astype(jnp.float32)
                send_buf[direction, distance - 1, half] = total.astype(jnp.bfloat16)
                piece(direction, distance, half).start()

    def finished(half):
        total = acc_ref[pl.ds(z * 8 + half * 4, 4)]
        for direction in range(2):
            total += recv_buf[direction, 0, half].astype(jnp.float32)
        return total.astype(jnp.bfloat16)

    for half in range(2):
        for direction in range(2):
            piece(direction, 1, half).wait_recv()
    give[...] = finished(other)
    handed = remote(give, out_ref.at[c], give_sem.at[0], give_sem.at[1], sibling)
    handed.start()
    out_ref[c] = finished(c)
    for distance in range(4, 0, -1):
        for half in range(2):
            for direction in range(2):
                if distance <= start[direction, half]:
                    piece(direction, distance, half).wait_send()
    handed.wait()


def scatter(acc):
    features = acc.shape[-1]
    vmem = pl.BlockSpec(memory_space=pltpu.VMEM)
    dma = pltpu.SemaphoreType.DMA
    ring = pltpu.VMEM((2, 4, 2, BLK_DEV, BLK, features), jnp.bfloat16)
    return pl.pallas_call(
        scatter_kernel,
        out_shape=jax.ShapeDtypeStruct((2, BLK_DEV, BLK, features), jnp.bfloat16),
        in_specs=[vmem],
        out_specs=vmem,
        scratch_shapes=[
            ring, ring,
            pltpu.VMEM((BLK_DEV, BLK, features), jnp.bfloat16),
            dma((2, 4, 2)), dma((2, 4, 2)), dma((2,)),
        ],
        compiler_params=pltpu.CompilerParams(
            collective_id=2, has_side_effects=True, vmem_limit_bytes=VMEM_LIMIT
        ),
        name="scatter_sums",
    )(acc)


def per_device(queries, key_rows, value_rows, out_grad, random_blocks, global_blocks):
    row_count, features = queries.shape
    blocks = (BLK_DEV, BLK, features)
    table = random_blocks.reshape(-1)
    k = key_rows.reshape(blocks)
    v = value_rows.reshape(blocks)
    slots, halo = gather(table, global_blocks, k, v)
    attended, query_grad, wacc, terms, rims = attend(
        queries.reshape(blocks), out_grad.reshape(blocks), k, v, halo, slots
    )
    everything, edges = spread_terms(terms, rims)
    total = scatter(land(table, global_blocks, everything))
    gradient = wacc + total.astype(jnp.float32)
    gradient = gradient.at[:, 0].add(edges[:, 0].astype(jnp.float32))
    gradient = gradient.at[:, BLK_DEV - 1].add(edges[:, 1].astype(jnp.float32))
    gradient = gradient.astype(jnp.bfloat16)
    return (
        attended.reshape(row_count, features),
        query_grad.reshape(row_count, features),
        gradient[0].reshape(row_count, features),
        gradient[1].reshape(row_count, features),
    )


def solution(mesh):
    in_specs = (
        P("seq", "head"),
        P("seq", "head"),
        P("seq", "head"),
        P("seq", "head"),
        P("head", None, None),
        P(),
    )
    out_specs = (P("seq", "head"), P("seq", "head"), P("seq", "head"), P("seq", "head"))
    return jax.shard_map(
        per_device, mesh=mesh, in_specs=in_specs, out_specs=out_specs, check_vma=False
    )
```

time: 606 us -> 254 us (0.42)
  waiting for transfers between devices: 445 us -> 0 us
  Pallas kernels: 0 us -> 249 us
  local copies, waits for them, and re-layouts: 63.2 us -> 2.44 us
  starting transfers between devices: 31.6 us -> 0 us
  other arithmetic: 25.6 us -> 1.41 us
  between operations: 19.7 us -> 0.71 us
  matrix products: 18.5 us -> 0 us
    psum x2 -> x0, waiting for transfers between devices: 275 us -> none  [the longest x1 225 us: spread(): return lax.psum(kept, axis)]
    pallas_call x0 -> x5, Pallas kernels: none -> 249 us  [the longest x1 115 us: gather(): pl.pallas_call(gather_kernel, out_shape=(jax.ShapeDtypeStruct((2, REQ + 2...]
    all_to_all x2 -> x0, waiting for transfers between devices: 152 us -> none  [the longest x1 152 us: per_device(): lax.all_to_all(returning, 'seq', split_axis=1, concat_axis=1, tiled=True)]
    all_to_all x2 -> x0, starting transfers between devices: 20.1 us -> none  [the longest x1 13.3 us: per_device(): lax.all_to_all(outgoing, 'seq', split_axis=1, concat_axis=1, tiled=True)]
    dot_general x8 -> x0, matrix products: 18.5 us -> none  [the longest x1 7.97 us: per_device(): jnp.einsum('sb,xskf->xbkf', landing, arrived, preferred_element_type=jnp....]
    ppermute x4 -> x0, waiting for transfers between devices: 17.3 us -> none  [the longest x2 8.68 us: with_halo(): lax.ppermute(lax.slice_in_dim(block, 0, width, axis=dim), axis, backward)]
    gather x4 -> x0, local copies, waits for them, and re-layouts: 16.2 us -> none  [the longest x1 6.72 us: per_device(): jnp.take(random_terms, source, axis=1)]
    select_n x7 -> x0, other arithmetic: 15.7 us -> none  [the longest x2 7.47 us: per_device(): jnp.take(random_terms, source, axis=1)]
  transfers between devices with their start and end apart: 8 -> 0, of which waited for: 5 -> 0; matrix products, arithmetic and copies ran while one was open for 4% -> 0% of each run, Pallas kernels for 0% -> 0%
where the time goes in v1:
time: 254 us
  Pallas kernels  249 us (98%)
    pallas_call x1, Pallas kernels, gather(): pl.pallas_call(gather_kernel, out_shape=(jax.ShapeDtypeStruct((2, REQ + 2...  115 us
    pallas_call x1, Pallas kernels, spread_terms(): pl.pallas_call(spread_kernel, out_shape=(jax.ShapeDtypeStruct((NX, SLOTS,...  65.5 us
    pallas_call x1, Pallas kernels, scatter(): pl.pallas_call(scatter_kernel, out_shape=jax.ShapeDtypeStruct((2, BLK_DEV...  50.3 us
    pallas_call x1, Pallas kernels, land(): pl.pallas_call(land_kernel, out_shape=jax.ShapeDtypeStruct((NZ * 8, BLK,...  9.62 us
    pallas_call x1, Pallas kernels, attend(): pl.pallas_call(attend_kernel, out_shape=(own, own, jax.ShapeDtypeStruct((...  8.28 us

profile of v1, /device:TPU:1, one launch (start us, length us, event | category | flops | bytes accessed | tf_op | source)
XLA Modules:
  0.0 253.6 jit_solution(1595441123971154987)
XLA Ops:
  0.6 0.8 copy.10
  1.4 0.8 reshape.101.table
  2.3 115.3 %gather_blocks.1 = (bf16[2,14,64,512]{3,2,1,0:T(8,128)(2,1)}, bf16[2,2,64,512]{3,2,1,0:T(8,128)(2,1)}) custom-call(s32[768]{0:T(1024)} %reshape.101.table, s32[2]{0:T(128)} %globals_.3, bf16[4,64,512]{2,1,0:T(8,128)(2,1)} %bitcast.8, bf16[4,64,512]{2,1,0:T(8,128)(2,1)} %bitcast.10), custom_call_target="tpu_custom_call" | custom-call | tf_op jit(solution)/shard_map/gather_blocks/pallas_call | solution.py:203
  117.6 8.3 %attend_blocks.1 = (bf16[4,64,512]{2,1,0:T(8,128)(2,1)}, bf16[4,64,512]{2,1,0:T(8,128)(2,1)}, f32[2,4,64,512]{3,2,1,0:T(8,128)}, bf16[2,14,64,512]{3,2,1,0:T(8,128)(2,1)}, bf16[2,2,64,512]{3,2,1,0:T(8,128)(2,1)}) custom-call(bf16[4,64,512]{2,1,0:T(8,128)(2,1)} %bitcast.12, bf16[4,64,512]{2,1,0:T(8,128)(2,1)} %bitcast.13, bf16[4,64,512]{2,1,0:T(8,128)(2,1)} %bitcast.9, ...), custom_call_target="tpu_custom_call" | custom-call | tf_op jit(solution)/shard_map/attend_blocks/pallas_call | solution.py:324
  125.9 65.5 %spread_terms.1 = (bf16[4,26,64,512]{3,2,1,0:T(8,128)(2,1)}, bf16[2,2,64,512]{3,2,1,0:T(8,128)(2,1)}) custom-call(bf16[2,14,64,512]{3,2,1,0:T(8,128)(2,1)} %get-tuple-element.42.term_ref, bf16[2,2,64,512]{3,2,1,0:T(8,128)(2,1)} %get-tuple-element.43.rim_ref), custom_call_target="tpu_custom_call" | custom-call | tf_op jit(solution)/shard_map/spread_terms/pallas_call | solution.py:422
  191.3 9.6 %land_terms.1.acc_ref = f32[64,64,512]{2,1,0:T(8,128)} custom-call(s32[768]{0:T(1024)} %reshape.101.table, s32[2]{0:T(128)} %globals_.3, bf16[4,26,64,512]{3,2,1,0:T(8,128)(2,1)} %get-tuple-element.44.all_ref), custom_call_target="tpu_custom_call" | custom-call | tf_op jit(solution)/shard_map/land_terms/pallas_call | solution.py:465
  200.9 0.0 copy-start
  201.0 0.0 copy-start.1
  201.0 50.3 %scatter_sums.1 = bf16[2,4,64,512]{3,2,1,0:T(8,128)(2,1)} custom-call(f32[64,64,512]{2,1,0:T(8,128)} %land_terms.1.acc_ref), custom_call_target="tpu_custom_call" | custom-call | tf_op jit(solution)/shard_map/scatter_sums/pallas_call | solution.py:531
  251.3 0.0 copy-done
  251.3 1.2 convert_add_fusion
  252.5 0.0 copy-done.1
  252.5 0.1 fusion.1
  252.6 0.1 fusion
  252.7 0.1 convert_element_type.17
  252.7 0.8 fusion.2
Async XLA Ops:
  200.9 50.3 %copy-start = (f32[2,4,64,512]{3,2,1,0:T(8,128)S(1)}, f32[2,4,64,512]{3,2,1,0:T(8,128)}, u32[]{:S(2)}) copy-start(f32[2,4,64,512]{3,2,1,0:T(8,128)} %get-tuple-element.41) | copy-start | bytes 3145732
  201.0 51.6 %copy-start.1 = (bf16[2,2,64,512]{3,2,1,0:T(8,128)(2,1)S(1)}, bf16[2,2,64,512]{3,2,1,0:T(8,128)(2,1)}, u32[]{:S(2)}) copy-start(bf16[2,2,64,512]{3,2,1,0:T(8,128)(2,1)} %get-tuple-element.45) | copy-start | bytes 786436

commit v2 on v1

v2 whole, which is shorter than its diff:
```python
import math

import jax
import jax.numpy as jnp
from jax import lax
from jax.experimental import pallas as pl
from jax.experimental.pallas import tpu as pltpu
from jax.sharding import PartitionSpec as P

HEAD_DIM = 128
BLK = 64
NZ = 8
NX = 4
NC = 2
NSEQ = NZ * NX * NC
BLK_DEV = 4
REQ = 12
SLOTS = 2 * REQ + 2
ENTRIES = NX * SLOTS
PARTS = 4
PART = 128
VMEM_LIMIT = 56 * 1024 * 1024


def seq_of(z, x, c):
    return (lax.rem(z + NZ, NZ) * NX + lax.rem(x + NX, NX)) * NC + c


def place():
    me = lax.axis_index("seq")
    z = me // (NX * NC)
    x = lax.rem(me // NC, NX)
    c = lax.rem(me, NC)
    return me, z, x, c


def remote(src, dst, send_sem, recv_sem, target):
    return pltpu.make_async_remote_copy(
        src_ref=src,
        dst_ref=dst,
        send_sem=send_sem,
        recv_sem=recv_sem,
        device_id={"seq": target},
        device_id_type=pl.DeviceIdType.MESH,
    )


def greet(partners):
    barrier = pltpu.get_barrier_semaphore()
    for partner in partners:
        pl.semaphore_signal(
            barrier, inc=1, device_id={"seq": partner}, device_id_type=pl.DeviceIdType.MESH
        )
    pl.semaphore_wait(barrier, len(partners))


def block_place(block):
    return lax.rem(lax.div(block, 8), NX), lax.div(block, 32) * 8 + lax.rem(block, 8)


Z_LAST = {(0, 0): 4, (0, 1): 3, (1, 0): 3, (1, 1): 4}


def gather_kernel(
    table, k_ref, v_ref, out_ref, halo_ref,
    s1_out, s1_in, s2_out, s2_in, s3_out, s3_in, give,
    pair_sem, halo_send, halo_recv, z_send, z_recv, x_send, x_recv, give_sem, *ag,
):
    me, z, x, c = place()
    other = 1 - c
    sibling = seq_of(z, x, other)
    after = lax.rem(me + 1, NSEQ)
    before = lax.rem(me + NSEQ - 1, NSEQ)
    sigma = 1 - 2 * c
    far = seq_of(z, x + sigma, c)
    near = seq_of(z, x - sigma, c)
    zs = (seq_of(z + 1, x, c), seq_of(z - 1, x, c))
    greet((after, before, zs[0], zs[1], far, near))

    def lanes(p):
        return pl.ds(p * PART, PART)

    def pair_copy(src, p):
        return remote(
            src.at[:, :, lanes(p)], ag[p].at[pl.ds(z * 8 + c * 4, 4)],
            pair_sem.at[0, p], pair_sem.at[1, p], sibling,
        )

    @pl.when(c == 0)
    def _():
        for p in range(PARTS):
            pair_copy(v_ref, p).start()
        for p in range(PARTS):
            ag[p][pl.ds(z * 8, 4)] = k_ref[:, :, p * PART : (p + 1) * PART]

    @pl.when(c == 1)
    def _():
        for p in range(PARTS):
            pair_copy(k_ref, p).start()
        for p in range(PARTS):
            ag[p][pl.ds(z * 8 + 4, 4)] = v_ref[:, :, p * PART : (p + 1) * PART]

    def z_piece(p, direction, step, half):
        origin = lax.rem(z + NZ - (step - 1), NZ) if direction == 0 else lax.rem(z + step - 1, NZ)
        piece = ag[p].at[pl.ds(origin * 8 + half * 4, 4)]
        return remote(
            piece,
            piece,
            z_send.at[p, direction, step - 1, half],
            z_recv.at[p, direction, step - 1, half],
            zs[direction],
        )

    def z_start(p):
        for direction in range(2):
            z_piece(p, direction, 1, c).start()
        pair_copy(v_ref, p).wait()
        for direction in range(2):
            z_piece(p, direction, 1, other).start()

    def z_step(p, step):
        for half in range(2):
            for direction in range(2):
                if step <= Z_LAST[direction, half]:
                    z_piece(p, direction, step, half).wait_recv()
                    if step + 1 <= Z_LAST[direction, half]:
                        z_piece(p, direction, step + 1, half).start()

    def wanted(p, chip, slot):
        source, at = block_place(table[(z * NX + lax.rem(chip + NX, NX)) * SLOTS + slot])
        return source, ag[p][at]

    def x_copy(p, number):
        src, dst, target = (
            (s1_out, s1_in, far), (s2_out, s2_in, far), (s3_out, s3_in, near)
        )[number]
        return remote(
            src.at[p], dst.at[p], x_send.at[p, number], x_recv.at[p, number], target
        )

    def x_first(p):
        @pl.loop(0, SLOTS, unroll=2)
        def _(slot):
            s1_out[p, slot] = wanted(p, x + 2, slot)[1]

        x_copy(p, 0).start()

        @pl.loop(0, SLOTS, unroll=2)
        def _(slot):
            s3_out[p, slot] = wanted(p, x - sigma, slot)[1]

        x_copy(p, 2).start()

    def x_second(p):
        x_copy(p, 0).wait_recv()

        @pl.loop(0, SLOTS, unroll=2)
        def _(slot):
            source, mine = wanted(p, x + sigma, slot)
            s2_out[p, slot] = jnp.where(source == x, mine, s1_in[p, slot])

        x_copy(p, 1).start()

    here = lax.rem(x + sigma + NX, NX)

    def chosen(p, slot):
        source, mine = wanted(p, x, slot)
        return jnp.where(
            source == x, mine, jnp.where(source == here, s3_in[p, slot], s2_in[p, slot])
        )

    def handed(p):
        return remote(
            give.at[p], out_ref.at[c, :, :, lanes(p)], give_sem.at[0, p], give_sem.at[1, p],
            sibling,
        )

    def finish(p):
        x_copy(p, 2).wait_recv()
        x_copy(p, 1).wait_recv()
        columns = slice(p * PART, (p + 1) * PART)

        @pl.loop(0, REQ, unroll=2)
        def _(i):
            give[p, i] = chosen(p, other * (REQ + 2) + i)

        for i in range(2):
            value = chosen(p, REQ + i)
            give[p, REQ + i] = value
            out_ref[c, REQ + i, :, columns] = value
        handed(p).start()

        @pl.loop(0, REQ, unroll=2)
        def _(i):
            out_ref[c, i, :, columns] = chosen(p, c * (REQ + 2) + i)

    halos = []
    for number, ref in enumerate((k_ref, v_ref)):
        for side, (row, target) in enumerate(((BLK_DEV - 1, after), (0, before))):
            halos.append(
                remote(
                    ref.at[row], halo_ref.at[number, side], halo_send.at[number, side],
                    halo_recv.at[number, side], target,
                )
            )

    z_start(0)
    for step in range(1, 5):
        z_step(0, step)
    if PARTS > 1:
        z_start(1)
    x_first(0)
    for p in range(PARTS):
        more = p + 1 < PARTS
        if more:
            z_step(p + 1, 1)
            z_step(p + 1, 2)
        x_second(p)
        if more:
            z_step(p + 1, 3)
            z_step(p + 1, 4)
            if p + 2 < PARTS:
                z_start(p + 2)
            x_first(p + 1)
        else:
            for copy in halos:
                copy.start()
        finish(p)

    for copy in halos:
        copy.wait()
    for p in range(PARTS):
        for (direction, half), last in Z_LAST.items():
            for step in range(1, last + 1):
                z_piece(p, direction, step, half).wait_send()
        for number in range(3):
            x_copy(p, number).wait_send()
        handed(p).wait()


def gather(table, k, v):
    features = k.shape[-1]
    big = pltpu.VMEM((PARTS, SLOTS, BLK, PART), jnp.bfloat16)
    vmem = pl.BlockSpec(memory_space=pltpu.VMEM)
    smem = pl.BlockSpec(memory_space=pltpu.SMEM)
    dma = pltpu.SemaphoreType.DMA
    return pl.pallas_call(
        gather_kernel,
        out_shape=(
            jax.ShapeDtypeStruct((2, REQ + 2, BLK, features), jnp.bfloat16),
            jax.ShapeDtypeStruct((2, 2, BLK, features), jnp.bfloat16),
        ),
        in_specs=[smem, vmem, vmem],
        out_specs=(vmem, vmem),
        scratch_shapes=[
            big, big, big, big, big, big,
            pltpu.VMEM((PARTS, REQ + 2, BLK, PART), jnp.bfloat16),
            dma((2, PARTS)), dma((2, 2)), dma((2, 2)), dma((PARTS, 2, 4, 2)), dma((PARTS, 2, 4, 2)),
            dma((PARTS, 3)), dma((PARTS, 3)), dma((2, PARTS)),
        ]
        + [pltpu.VMEM((NZ * 8, BLK, PART), jnp.bfloat16)] * PARTS,
        compiler_params=pltpu.CompilerParams(
            collective_id=0, has_side_effects=True, vmem_limit_bytes=VMEM_LIMIT
        ),
        name="gather_blocks",
    )(table, k, v)


def nt(a, b):
    return lax.dot_general(a, b, (((1,), (1,)), ((), ())), preferred_element_type=jnp.float32)


def tn(a, b):
    return lax.dot_general(a, b, (((0,), (0,)), ((), ())), preferred_element_type=jnp.float32)


def nn(a, b):
    return lax.dot_general(a, b, (((1,), (0,)), ((), ())), preferred_element_type=jnp.float32)


def attend_kernel(
    q_ref, g_ref, k_ref, v_ref, halo_ref, slot_ref,
    att_ref, qg_ref, wacc_ref, term_ref, rim_ref, acc, gacc,
):
    me = lax.axis_index("seq")
    features = q_ref.shape[-1]
    heads = features // HEAD_DIM
    scale = 1.0 / math.sqrt(HEAD_DIM)
    lane_head = lax.broadcasted_iota(jnp.int32, (BLK, features), 1) // HEAD_DIM
    acc[...] = jnp.zeros_like(acc)
    gacc[...] = jnp.zeros_like(gacc)

    def spread(rows):
        zero = jnp.zeros_like(rows)
        return jnp.concatenate(
            [jnp.where(lane_head == h, rows, zero) for h in range(heads)], axis=0
        )

    def diagonal(full):
        return jnp.concatenate(
            [
                full[h * BLK : (h + 1) * BLK, h * HEAD_DIM : (h + 1) * HEAD_DIM]
                for h in range(heads)
            ],
            axis=1,
        )

    for b in range(BLK_DEV):
        def listed(number, own):
            window = [
                halo_ref[number, 0] if b == 0 else own[b - 1],
                own[b],
                halo_ref[number, 1] if b == BLK_DEV - 1 else own[b + 1],
            ]
            extra = [slot_ref[number, REQ], slot_ref[number, REQ + 1]]
            random = [slot_ref[number, 3 * b + i] for i in range(3)]
            return jnp.concatenate(window + extra + random, axis=0)

        keys = listed(0, k_ref)
        values = listed(1, v_ref)
        query = spread(q_ref[b])
        grad = spread(g_ref[b])
        scores = nt(keys, query) * scale
        if b == 0:
            scores = jnp.concatenate(
                [jnp.where(me == 0, -jnp.inf, scores[:BLK]), scores[BLK:]], axis=0
            )
        if b == BLK_DEV - 1:
            scores = jnp.concatenate(
                [
                    scores[: 2 * BLK],
                    jnp.where(me == NSEQ - 1, -jnp.inf, scores[2 * BLK : 3 * BLK]),
                    scores[3 * BLK :],
                ],
                axis=0,
            )
        row_max = jnp.max(scores, axis=0, keepdims=True)
        raw = jnp.exp(scores - row_max)
        weights = raw * (1.0 / jnp.sum(raw, axis=0, keepdims=True))
        weights_b = weights.astype(jnp.bfloat16)
        weight_grads = nt(values, grad)
        row_dot = jnp.sum(weights_b.astype(jnp.float32) * weight_grads, axis=0, keepdims=True)
        score_grads = (weights * (weight_grads - row_dot) * scale).astype(jnp.bfloat16)
        att_ref[b] = diagonal(tn(weights_b, values)).astype(jnp.bfloat16)
        qg_ref[b] = diagonal(tn(score_grads, keys)).astype(jnp.bfloat16)
        for number, terms in enumerate((nn(score_grads, query), nn(weights_b, grad))):
            for i in range(3):
                acc[number, b + i] += terms[i * BLK : (i + 1) * BLK]
            for i in range(2):
                gacc[number, i] += terms[(3 + i) * BLK : (4 + i) * BLK]
            for i in range(3):
                term_ref[number, 3 * b + i] = terms[(5 + i) * BLK : (6 + i) * BLK].astype(
                    jnp.bfloat16
                )
    for number in range(2):
        for i in range(2):
            term_ref[number, REQ + i] = gacc[number, i].astype(jnp.bfloat16)
        rim_ref[number, 0] = acc[number, 0].astype(jnp.bfloat16)
        rim_ref[number, 1] = acc[number, BLK_DEV + 1].astype(jnp.bfloat16)
        for i in range(BLK_DEV):
            wacc_ref[number, i] = acc[number, i + 1]


def attend(q, g, k, v, halo, slots):
    features = q.shape[-1]
    vmem = pl.BlockSpec(memory_space=pltpu.VMEM)
    own = jax.ShapeDtypeStruct((BLK_DEV, BLK, features), jnp.bfloat16)
    return pl.pallas_call(
        attend_kernel,
        out_shape=(
            own,
            own,
            jax.ShapeDtypeStruct((2, BLK_DEV, BLK, features), jnp.float32),
            jax.ShapeDtypeStruct((2, REQ + 2, BLK, features), jnp.bfloat16),
            jax.ShapeDtypeStruct((2, 2, BLK, features), jnp.bfloat16),
        ),
        in_specs=[vmem] * 6,
        out_specs=(vmem,) * 5,
        scratch_shapes=[
            pltpu.VMEM((2, BLK_DEV + 2, BLK, features), jnp.float32),
            pltpu.VMEM((2, 2, BLK, features), jnp.float32),
        ],
        compiler_params=pltpu.CompilerParams(vmem_limit_bytes=VMEM_LIMIT),
        name="attend_blocks",
    )(q, g, k, v, halo, slots)


def plan_kernel(table, prev_ref, last_ref):
    me, z, x, c = place()

    @pl.loop(0, NZ * 8)
    def _(at):
        last_ref[at] = ENTRIES

    @pl.loop(0, ENTRIES)
    def _(n):
        source, at = block_place(table[z * ENTRIES + n])
        prev_ref[n] = ENTRIES

        @pl.when(source == x)
        def _():
            prev_ref[n] = last_ref[at]
            last_ref[at] = n


def plan(table):
    smem = pl.BlockSpec(memory_space=pltpu.SMEM)
    return pl.pallas_call(
        plan_kernel,
        out_shape=(
            jax.ShapeDtypeStruct((ENTRIES,), jnp.int32),
            jax.ShapeDtypeStruct((NZ * 8,), jnp.int32),
        ),
        in_specs=[smem],
        out_specs=(smem, smem),
        name="plan_sums",
    )(table)


def back_kernel(
    prev, last, term_ref, rim_ref, out_ref, edge_ref,
    theirs, everything, chain, landed, send_buf, recv_buf, give,
    pair_sem, rim_send, rim_recv, x_send, x_recv, z_send, z_recv, give_sem,
):
    me, z, x, c = place()
    other = 1 - c
    sibling = seq_of(z, x, other)
    after = lax.rem(me + 1, NSEQ)
    before = lax.rem(me + NSEQ - 1, NSEQ)
    sigma = 1 - 2 * c
    xs = (seq_of(z, x + sigma, c), seq_of(z, x - sigma, c))
    zs = (seq_of(z + 1, x, c), seq_of(z - 1, x, c))
    greet((after, before, xs[0], xs[1], zs[0], zs[1]))

    def lanes(p):
        return pl.ds(p * PART, PART)

    def pair(p):
        return remote(
            term_ref.at[other, :, :, lanes(p)], theirs.at[p], pair_sem.at[0, p],
            pair_sem.at[1, p], sibling,
        )

    for p in range(PARTS):
        pair(p).start()

    def own(p, chip):
        base = lax.rem(chip + NX, NX) * SLOTS
        return everything.at[p, pl.ds(base + c * (REQ + 2), REQ)]

    def rest(p, chip):
        base = lax.rem(chip + NX, NX) * SLOTS
        return everything.at[p, pl.ds(base + other * REQ, REQ + 2)]

    def send(p, number, chip, which):
        ref = (own, rest)[which](p, chip)
        return remote(
            ref, ref, x_send.at[p, number, which], x_recv.at[p, number, which],
            xs[(0, 1, 0)[number]],
        )

    def x_first(p):
        columns = slice(p * PART, (p + 1) * PART)
        base = x * SLOTS

        @pl.loop(0, REQ, unroll=2)
        def _(i):
            everything[p, base + c * (REQ + 2) + i] = term_ref[c, i, :, columns]

        for number in range(2):
            send(p, number, x, 0).start()
        pair(p).wait_recv()

        @pl.loop(0, REQ, unroll=2)
        def _(i):
            everything[p, base + other * (REQ + 2) + i] = theirs[p, i]

        for i in range(2):
            total = term_ref[c, REQ + i, :, columns].astype(jnp.float32) + theirs[
                p, REQ + i
            ].astype(jnp.float32)
            everything[p, base + REQ + i] = total.astype(jnp.bfloat16)
        for number in range(2):
            send(p, number, x, 1).start()

    def x_second(p):
        for which in range(2):
            send(p, 0, x - sigma, which).wait_recv()
            send(p, 2, x - sigma, which).start()

    def x_wait(p, number):
        for which in range(2):
            send(p, number, x, which).wait_recv()

    chain[ENTRIES] = jnp.zeros((BLK, PART), jnp.float32)

    def land(p):
        @pl.loop(0, ENTRIES, unroll=4)
        def _(n):
            chain[n] = everything[p, n].astype(jnp.float32) + chain[prev[n]]

        @pl.loop(0, NZ * 8, unroll=4)
        def _(at):
            landed[p, at] = chain[last[at]]

    def piece(p, direction, distance, half):
        return remote(
            send_buf.at[p, direction, distance - 1, half],
            recv_buf.at[p, direction, distance - 1, half],
            z_send.at[p, direction, distance - 1, half],
            z_recv.at[p, direction, distance - 1, half],
            zs[direction],
        )

    def z_step(p, distance):
        for half in range(2):
            for direction in range(2):
                if distance > Z_LAST[direction, half]:
                    continue
                target = lax.rem(z + (distance if direction == 0 else NZ - distance), NZ)
                first = target * 8 + half * 4
                waits = distance < Z_LAST[direction, half]
                if waits:
                    piece(p, direction, distance + 1, half).wait_recv()
                for i in range(BLK_DEV):
                    total = landed[p, first + i]
                    if waits:
                        total += recv_buf[p, direction, distance, half, i].astype(jnp.float32)
                    send_buf[p, direction, distance - 1, half, i] = total.astype(jnp.bfloat16)
                piece(p, direction, distance, half).start()

    def handed(p):
        return remote(
            give.at[p], out_ref.at[c, :, :, lanes(p)], give_sem.at[0, p], give_sem.at[1, p],
            sibling,
        )

    def finish(p):
        columns = slice(p * PART, (p + 1) * PART)
        for half in range(2):
            for direction in range(2):
                piece(p, direction, 1, half).wait_recv()

        def finished(half, i):
            total = landed[p, z * 8 + half * 4 + i]
            for direction in range(2):
                total += recv_buf[p, direction, 0, half, i].astype(jnp.float32)
            return total.astype(jnp.bfloat16)

        for i in range(BLK_DEV):
            give[p, i] = finished(other, i)
        handed(p).start()
        for i in range(BLK_DEV):
            out_ref[c, i, :, columns] = finished(c, i)

    edges = []
    for number in range(2):
        for side, target in enumerate((after, before)):
            edges.append(
                remote(
                    rim_ref.at[number, 1 - side], edge_ref.at[number, side],
                    rim_send.at[number, side], rim_recv.at[number, side], target,
                )
            )

    x_first(0)
    for p in range(PARTS):
        x_second(p)
        if p + 1 < PARTS:
            x_first(p + 1)
        else:
            for copy in edges:
                copy.start()
        if p:
            z_step(p - 1, 3)
        x_wait(p, 1)
        if p:
            z_step(p - 1, 2)
        x_wait(p, 2)
        if p:
            z_step(p - 1, 1)
        land(p)
        z_step(p, 4)
        if p:
            finish(p - 1)
    for distance in (3, 2, 1):
        z_step(PARTS - 1, distance)
    finish(PARTS - 1)

    for copy in edges:
        copy.wait()
    for p in range(PARTS):
        pair(p).wait_send()
        for number in range(3):
            for which in range(2):
                send(p, number, x, which).wait_send()
        for (direction, half), most in Z_LAST.items():
            for distance in range(1, most + 1):
                piece(p, direction, distance, half).wait_send()
        handed(p).wait()


def send_back(prev, last, terms, rims):
    features = terms.shape[-1]
    vmem = pl.BlockSpec(memory_space=pltpu.VMEM)
    smem = pl.BlockSpec(memory_space=pltpu.SMEM)
    dma = pltpu.SemaphoreType.DMA
    ring = pltpu.VMEM((PARTS, 2, 4, 2, BLK_DEV, BLK, PART), jnp.bfloat16)
    return pl.pallas_call(
        back_kernel,
        out_shape=(
            jax.ShapeDtypeStruct((2, BLK_DEV, BLK, features), jnp.bfloat16),
            jax.ShapeDtypeStruct((2, 2, BLK, features), jnp.bfloat16),
        ),
        in_specs=[smem, smem, vmem, vmem],
        out_specs=(vmem, vmem),
        scratch_shapes=[
            pltpu.VMEM((PARTS, REQ + 2, BLK, PART), jnp.bfloat16),
            pltpu.VMEM((PARTS, ENTRIES, BLK, PART), jnp.bfloat16),
            pltpu.VMEM((ENTRIES + 1, BLK, PART), jnp.float32),
            pltpu.VMEM((PARTS, NZ * 8, BLK, PART), jnp.float32),
            ring, ring,
            pltpu.VMEM((PARTS, BLK_DEV, BLK, PART), jnp.bfloat16),
            dma((2, PARTS)), dma((2, 2)), dma((2, 2)), dma((PARTS, 3, 2)), dma((PARTS, 3, 2)),
            dma((PARTS, 2, 4, 2)), dma((PARTS, 2, 4, 2)), dma((2, PARTS)),
        ],
        compiler_params=pltpu.CompilerParams(
            collective_id=1, has_side_effects=True, vmem_limit_bytes=VMEM_LIMIT
        ),
        name="send_back",
    )(prev, last, terms, rims)


def per_device(queries, key_rows, value_rows, out_grad, random_blocks, global_blocks):
    row_count, features = queries.shape
    blocks = (BLK_DEV, BLK, features)
    lists = random_blocks.reshape(NZ * NX, NC, REQ)
    shared = jnp.broadcast_to(global_blocks[None], (NZ * NX, 2))
    table = jnp.concatenate([lists[:, 0], shared, lists[:, 1]], axis=1).reshape(-1)
    k = key_rows.reshape(blocks)
    v = value_rows.reshape(blocks)
    prev, last = plan(table)
    slots, halo = gather(table, k, v)
    attended, query_grad, wacc, terms, rims = attend(
        queries.reshape(blocks), out_grad.reshape(blocks), k, v, halo, slots
    )
    total, edges = send_back(prev, last, terms, rims)
    gradient = wacc + total.astype(jnp.float32)
    gradient = gradient.at[:, 0].add(edges[:, 0].astype(jnp.float32))
    gradient = gradient.at[:, BLK_DEV - 1].add(edges[:, 1].astype(jnp.float32))
    gradient = gradient.astype(jnp.bfloat16)
    return (
        attended.reshape(row_count, features),
        query_grad.reshape(row_count, features),
        gradient[0].reshape(row_count, features),
        gradient[1].reshape(row_count, features),
    )


def solution(mesh):
    in_specs = (
        P("seq", "head"),
        P("seq", "head"),
        P("seq", "head"),
        P("seq", "head"),
        P("head", None, None),
        P(),
    )
    out_specs = (P("seq", "head"), P("seq", "head"), P("seq", "head"), P("seq", "head"))
    return jax.shard_map(
        per_device, mesh=mesh, in_specs=in_specs, out_specs=out_specs, check_vma=False
    )
```

time: 254 us -> 209 us (0.82)
  Pallas kernels: 249 us -> 203 us
    pallas_call x3 -> x2, Pallas kernels: 125 us -> 95 us  [the longest x1 91.5 us: send_back(): pl.pallas_call(back_kernel, out_shape=(jax.ShapeDtypeStruct((2, BLK_DEV,...]
    pallas_call x1, Pallas kernels: 115 us -> 99.7 us  [gather(): pl.pallas_call(gather_kernel, out_shape=(jax.ShapeDtypeStruct((2, REQ + 2...]
where the time goes in v2:
time: 209 us; the launch traced here: 208 us
  Pallas kernels  203 us (97%)
  local copies, waits for them, and re-layouts  3.2 us (2%)
    pallas_call x1, Pallas kernels, gather(): pl.pallas_call(gather_kernel, out_shape=(jax.ShapeDtypeStruct((2, REQ + 2...  99.7 us
    pallas_call x1, Pallas kernels, send_back(): pl.pallas_call(back_kernel, out_shape=(jax.ShapeDtypeStruct((2, BLK_DEV,...  91.5 us
    pallas_call x1, Pallas kernels, attend(): pl.pallas_call(attend_kernel, out_shape=(own, own, jax.ShapeDtypeStruct((...  8.28 us

profile of v2, /device:TPU:1, one launch (start us, length us, event | category | flops | bytes accessed | tf_op | source)
XLA Modules:
  0.0 208.5 jit_solution(15893817995084284296)
XLA Ops:
  0.6 0.7 pad.5.clone
  1.4 0.8 copy.11
  2.2 0.1 reshape.105
  2.3 0.1 pad_add_fusion
  2.4 0.7 reshape.106.table
  3.1 3.6 %plan_sums.1 = (s32[104]{0:T(128)}, s32[64]{0:T(128)}) custom-call(s32[832]{0:T(1024)} %reshape.106.table), custom_call_target="tpu_custom_call" | custom-call | tf_op jit(solution)/shard_map/plan_sums/pallas_call | solution.py:408
  6.7 99.7 %gather_blocks.1 = (bf16[2,14,64,512]{3,2,1,0:T(8,128)(2,1)}, bf16[2,2,64,512]{3,2,1,0:T(8,128)(2,1)}) custom-call(s32[832]{0:T(1024)} %reshape.106.table, bf16[4,64,512]{2,1,0:T(8,128)(2,1)} %bitcast.12, bf16[4,64,512]{2,1,0:T(8,128)(2,1)} %bitcast.14), custom_call_target="tpu_custom_call" | custom-call | tf_op jit(solution)/shard_map/gather_blocks/pallas_call | solution.py:247
  106.4 8.3 %attend_blocks.1 = (bf16[4,64,512]{2,1,0:T(8,128)(2,1)}, bf16[4,64,512]{2,1,0:T(8,128)(2,1)}, f32[2,4,64,512]{3,2,1,0:T(8,128)}, bf16[2,14,64,512]{3,2,1,0:T(8,128)(2,1)}, bf16[2,2,64,512]{3,2,1,0:T(8,128)(2,1)}) custom-call(bf16[4,64,512]{2,1,0:T(8,128)(2,1)} %bitcast.16, bf16[4,64,512]{2,1,0:T(8,128)(2,1)} %bitcast.17, bf16[4,64,512]{2,1,0:T(8,128)(2,1)} %bitcast.13, ...), custom_call_target="tpu_custom_call" | custom-call | tf_op jit(solution)/shard_map/attend_blocks/pallas_call | solution.py:368
  114.7 0.0 copy-start
  114.7 91.5 %send_back.1 = (bf16[2,4,64,512]{3,2,1,0:T(8,128)(2,1)}, bf16[2,2,64,512]{3,2,1,0:T(8,128)(2,1)}) custom-call(s32[104]{0:T(128)} %get-tuple-element.44.prev, s32[64]{0:T(128)} %get-tuple-element.45.last, bf16[2,14,64,512]{3,2,1,0:T(8,128)(2,1)} %get-tuple-element.46.term_ref, bf16[2,2,64,512]{3,2,1,0:T(8,128)(2,1)} %get-tuple-element.47.rim_ref), custom_call_target="tpu_custom_call" | custom-call | tf_op jit(solution)/shard_map/send_back/pallas_call | solution.py:609
  206.1 0.0 copy-start.1
  206.1 0.0 copy-done
  206.1 1.3 convert_add_fusion
  207.4 0.0 copy-done.1
  207.4 0.1 fusion.1
  207.5 0.1 fusion
  207.6 0.1 convert_element_type.17
  207.6 0.8 fusion.2
  (1 shorter events, 0.0 us)
Async XLA Ops:
  114.7 91.5 %copy-start = (f32[2,4,64,512]{3,2,1,0:T(8,128)S(1)}, f32[2,4,64,512]{3,2,1,0:T(8,128)}, u32[]{:S(2)}) copy-start(f32[2,4,64,512]{3,2,1,0:T(8,128)} %get-tuple-element.43) | copy-start | bytes 3145732
  206.1 1.3 copy-start.1

commit v3 on v2

--- a/solution.py
+++ b/solution.py
@@ -19,6 +19,7 @@
 ENTRIES = NX * SLOTS
 PARTS = 4
 PART = 128
+ROWS = BLK // 2
 VMEM_LIMIT = 56 * 1024 * 1024
 
 
@@ -71,11 +72,9 @@
     sibling = seq_of(z, x, other)
     after = lax.rem(me + 1, NSEQ)
     before = lax.rem(me + NSEQ - 1, NSEQ)
-    sigma = 1 - 2 * c
-    far = seq_of(z, x + sigma, c)
-    near = seq_of(z, x - sigma, c)
+    xs = (seq_of(z, x + 1, c), seq_of(z, x - 1, c))
     zs = (seq_of(z + 1, x, c), seq_of(z - 1, x, c))
-    greet((after, before, zs[0], zs[1], far, near))
+    greet((after, before, zs[0], zs[1], xs[0], xs[1]))
 
     def lanes(p):
         return pl.ds(p * PART, PART)
@@ -130,44 +129,52 @@
         source, at = block_place(table[(z * NX + lax.rem(chip + NX, NX)) * SLOTS + slot])
         return source, ag[p][at]
 
-    def x_copy(p, number):
-        src, dst, target = (
-            (s1_out, s1_in, far), (s2_out, s2_in, far), (s3_out, s3_in, near)
-        )[number]
-        return remote(
-            src.at[p], dst.at[p], x_send.at[p, number], x_recv.at[p, number], target
+    def x_copy(p, number, g):
+        src, dst, way = ((s1_out, s1_in, g), (s2_out, s2_in, g), (s3_out, s3_in, 1 - g))[number]
+        return remote(
+            src.at[p, g], dst.at[p, g], x_send.at[p, number, g], x_recv.at[p, number, g], xs[way]
         )
 
     def x_first(p):
         @pl.loop(0, SLOTS, unroll=2)
         def _(slot):
-            s1_out[p, slot] = wanted(p, x + 2, slot)[1]
-
-        x_copy(p, 0).start()
+            mine = wanted(p, x + 2, slot)[1]
+            s1_out[p, 0, slot] = mine[:ROWS]
+            s1_out[p, 1, slot] = mine[ROWS:]
+
+        for g in range(2):
+            x_copy(p, 0, g).start()
 
         @pl.loop(0, SLOTS, unroll=2)
         def _(slot):
-            s3_out[p, slot] = wanted(p, x - sigma, slot)[1]
-
-        x_copy(p, 2).start()
+            s3_out[p, 0, slot] = wanted(p, x - 1, slot)[1][:ROWS]
+            s3_out[p, 1, slot] = wanted(p, x + 1, slot)[1][ROWS:]
+
+        for g in range(2):
+            x_copy(p, 2, g).start()
 
     def x_second(p):
-        x_copy(p, 0).wait_recv()
+        for g in range(2):
+            x_copy(p, 0, g).wait_recv()
 
         @pl.loop(0, SLOTS, unroll=2)
         def _(slot):
-            source, mine = wanted(p, x + sigma, slot)
-            s2_out[p, slot] = jnp.where(source == x, mine, s1_in[p, slot])
-
-        x_copy(p, 1).start()
-
-    here = lax.rem(x + sigma + NX, NX)
+            source, mine = wanted(p, x + 1, slot)
+            s2_out[p, 0, slot] = jnp.where(source == x, mine[:ROWS], s1_in[p, 0, slot])
+            source, mine = wanted(p, x - 1, slot)
+            s2_out[p, 1, slot] = jnp.where(source == x, mine[ROWS:], s1_in[p, 1, slot])
+
+        for g in range(2):
+            x_copy(p, 1, g).start()
+
+    here = (lax.rem(x + 1, NX), lax.rem(x + NX - 1, NX))
 
     def chosen(p, slot):
         source, mine = wanted(p, x, slot)
-        return jnp.where(
-            source == x, mine, jnp.where(source == here, s3_in[p, slot], s2_in[p, slot])
-        )
+        passed = [
+            jnp.where(source == here[g], s3_in[p, g, slot], s2_in[p, g, slot]) for g in range(2)
+        ]
+        return jnp.where(source == x, mine, jnp.concatenate(passed, axis=0))
 
     def handed(p):
         return remote(
@@ -176,8 +183,9 @@
         )
 
     def finish(p):
-        x_copy(p, 2).wait_recv()
-        x_copy(p, 1).wait_recv()
+        for number in (2, 1):
+            for g in range(2):
+                x_copy(p, number, g).wait_recv()
         columns = slice(p * PART, (p + 1) * PART)
 
         @pl.loop(0, REQ, unroll=2)
@@ -234,13 +242,14 @@
             for step in range(1, last + 1):
                 z_piece(p, direction, step, half).wait_send()
         for number in range(3):
-            x_copy(p, number).wait_send()
+            for g in range(2):
+                x_copy(p, number, g).wait_send()
         handed(p).wait()
 
 
 def gather(table, k, v):
     features = k.shape[-1]
-    big = pltpu.VMEM((PARTS, SLOTS, BLK, PART), jnp.bfloat16)
+    big = pltpu.VMEM((PARTS, 2, SLOTS, ROWS, PART), jnp.bfloat16)
     vmem = pl.BlockSpec(memory_space=pltpu.VMEM)
     smem = pl.BlockSpec(memory_space=pltpu.SMEM)
     dma = pltpu.SemaphoreType.DMA
@@ -256,7 +265,7 @@
             big, big, big, big, big, big,
             pltpu.VMEM((PARTS, REQ + 2, BLK, PART), jnp.bfloat16),
             dma((2, PARTS)), dma((2, 2)), dma((2, 2)), dma((PARTS, 2, 4, 2)), dma((PARTS, 2, 4, 2)),
-            dma((PARTS, 3)), dma((PARTS, 3)), dma((2, PARTS)),
+            dma((PARTS, 3, 2)), dma((PARTS, 3, 2)), dma((2, PARTS)),
         ]
         + [pltpu.VMEM((NZ * 8, BLK, PART), jnp.bfloat16)] * PARTS,
         compiler_params=pltpu.CompilerParams(
@@ -427,8 +436,7 @@
     sibling = seq_of(z, x, other)
     after = lax.rem(me + 1, NSEQ)
     before = lax.rem(me + NSEQ - 1, NSEQ)
-    sigma = 1 - 2 * c
-    xs = (seq_of(z, x + sigma, c), seq_of(z, x - sigma, c))
+    xs = (seq_of(z, x + 1, c), seq_of(z, x - 1, c))
     zs = (seq_of(z + 1, x, c), seq_of(z - 1, x, c))
     greet((after, before, xs[0], xs[1], zs[0], zs[1]))
 
@@ -444,19 +452,19 @@
     for p in range(PARTS):
         pair(p).start()
 
-    def own(p, chip):
+    def own(p, chip, g):
         base = lax.rem(chip + NX, NX) * SLOTS
-        return everything.at[p, pl.ds(base + c * (REQ + 2), REQ)]
-
-    def rest(p, chip):
+        return everything.at[p, pl.ds(base + c * (REQ + 2), REQ), pl.ds(g * ROWS, ROWS)]
+
+    def rest(p, chip, g):
         base = lax.rem(chip + NX, NX) * SLOTS
-        return everything.at[p, pl.ds(base + other * REQ, REQ + 2)]
-
-    def send(p, number, chip, which):
-        ref = (own, rest)[which](p, chip)
-        return remote(
-            ref, ref, x_send.at[p, number, which], x_recv.at[p, number, which],
-            xs[(0, 1, 0)[number]],
+        return everything.at[p, pl.ds(base + other * REQ, REQ + 2), pl.ds(g * ROWS, ROWS)]
+
+    def send(p, number, chip, which, g):
+        ref = (own, rest)[which](p, chip, g)
+        return remote(
+            ref, ref, x_send.at[p, number, which, g], x_recv.at[p, number, which, g],
+            xs[(g, 1 - g, g)[number]],
         )
 
     def x_first(p):
@@ -468,7 +476,8 @@
             everything[p, base + c * (REQ + 2) + i] = term_ref[c, i, :, columns]
 
         for number in range(2):
-            send(p, number, x, 0).start()
+            for g in range(2):
+                send(p, number, x, 0, g).start()
         pair(p).wait_recv()
 
         @pl.loop(0, REQ, unroll=2)
@@ -481,16 +490,19 @@
             ].astype(jnp.float32)
             everything[p, base + REQ + i] = total.astype(jnp.bfloat16)
         for number in range(2):
-            send(p, number, x, 1).start()
+            for g in range(2):
+                send(p, number, x, 1, g).start()
 
     def x_second(p):
         for which in range(2):
-            send(p, 0, x - sigma, which).wait_recv()
-            send(p, 2, x - sigma, which).start()
+            for g, behind in enumerate((x - 1, x + 1)):
+                send(p, 0, behind, which, g).wait_recv()
+                send(p, 2, behind, which, g).start()
 
     def x_wait(p, number):
         for which in range(2):
-            send(p, number, x, which).wait_recv()
+            for g in range(2):
+                send(p, number, x, which, g).wait_recv()
 
     chain[ENTRIES] = jnp.zeros((BLK, PART), jnp.float32)
 
@@ -593,7 +605,8 @@
         pair(p).wait_send()
         for number in range(3):
             for which in range(2):
-                send(p, number, x, which).wait_send()
+                for g in range(2):
+                    send(p, number, x, which, g).wait_send()
         for (direction, half), most in Z_LAST.items():
             for distance in range(1, most + 1):
                 piece(p, direction, distance, half).wait_send()
@@ -621,7 +634,7 @@
             pltpu.VMEM((PARTS, NZ * 8, BLK, PART), jnp.float32),
             ring, ring,
             pltpu.VMEM((PARTS, BLK_DEV, BLK, PART), jnp.bfloat16),
-            dma((2, PARTS)), dma((2, 2)), dma((2, 2)), dma((PARTS, 3, 2)), dma((PARTS, 3, 2)),
+            dma((2, PARTS)), dma((2, 2)), dma((2, 2)), dma((PARTS, 3, 2, 2)), dma((PARTS, 3, 2, 2)),
             dma((PARTS, 2, 4, 2)), dma((PARTS, 2, 4, 2)), dma((2, PARTS)),
         ],
         compiler_params=pltpu.CompilerParams(

time: 209 us -> 201 us (0.962)
  Pallas kernels: 203 us -> 195 us
    pallas_call x1, Pallas kernels: 99.7 us -> 93.5 us  [gather(): pl.pallas_call(gather_kernel, out_shape=(jax.ShapeDtypeStruct((2, REQ + 2...]
where the time goes in v3:
time: 201 us
  Pallas kernels  195 us (97%)
  local copies, waits for them, and re-layouts  3.2 us (2%)
    pallas_call x1, Pallas kernels, gather(): pl.pallas_call(gather_kernel, out_shape=(jax.ShapeDtypeStruct((2, REQ + 2...  93.5 us
    pallas_call x1, Pallas kernels, send_back(): pl.pallas_call(back_kernel, out_shape=(jax.ShapeDtypeStruct((2, BLK_DEV,...  89.7 us
    pallas_call x1, Pallas kernels, attend(): pl.pallas_call(attend_kernel, out_shape=(own, own, jax.ShapeDtypeStruct((...  8.28 us

profile of v3, /device:TPU:1, one launch (start us, length us, event | category | flops | bytes accessed | tf_op | source)
XLA Modules:
  0.0 200.6 jit_solution(17671029846354502035)
XLA Ops:
  0.6 0.7 pad.5.clone
  1.4 0.8 copy.11
  2.2 0.1 reshape.105
  2.3 0.1 pad_add_fusion
  2.4 0.7 reshape.106.table
  3.1 3.6 %plan_sums.1 = (s32[104]{0:T(128)}, s32[64]{0:T(128)}) custom-call(s32[832]{0:T(1024)} %reshape.106.table), custom_call_target="tpu_custom_call" | custom-call | tf_op jit(solution)/shard_map/plan_sums/pallas_call | solution.py:417
  6.7 93.5 %gather_blocks.1 = (bf16[2,14,64,512]{3,2,1,0:T(8,128)(2,1)}, bf16[2,2,64,512]{3,2,1,0:T(8,128)(2,1)}) custom-call(s32[832]{0:T(1024)} %reshape.106.table, bf16[4,64,512]{2,1,0:T(8,128)(2,1)} %bitcast.12, bf16[4,64,512]{2,1,0:T(8,128)(2,1)} %bitcast.14), custom_call_target="tpu_custom_call" | custom-call | tf_op jit(solution)/shard_map/gather_blocks/pallas_call | solution.py:256
  100.2 8.3 %attend_blocks.1 = (bf16[4,64,512]{2,1,0:T(8,128)(2,1)}, bf16[4,64,512]{2,1,0:T(8,128)(2,1)}, f32[2,4,64,512]{3,2,1,0:T(8,128)}, bf16[2,14,64,512]{3,2,1,0:T(8,128)(2,1)}, bf16[2,2,64,512]{3,2,1,0:T(8,128)(2,1)}) custom-call(bf16[4,64,512]{2,1,0:T(8,128)(2,1)} %bitcast.16, bf16[4,64,512]{2,1,0:T(8,128)(2,1)} %bitcast.17, bf16[4,64,512]{2,1,0:T(8,128)(2,1)} %bitcast.13, ...), custom_call_target="tpu_custom_call" | custom-call | tf_op jit(solution)/shard_map/attend_blocks/pallas_call | solution.py:377
  108.5 0.0 copy-start
  108.5 89.7 %send_back.1 = (bf16[2,4,64,512]{3,2,1,0:T(8,128)(2,1)}, bf16[2,2,64,512]{3,2,1,0:T(8,128)(2,1)}) custom-call(s32[104]{0:T(128)} %get-tuple-element.44.prev, s32[64]{0:T(128)} %get-tuple-element.45.last, bf16[2,14,64,512]{3,2,1,0:T(8,128)(2,1)} %get-tuple-element.46.term_ref, bf16[2,2,64,512]{3,2,1,0:T(8,128)(2,1)} %get-tuple-element.47.rim_ref), custom_call_target="tpu_custom_call" | custom-call | tf_op jit(solution)/shard_map/send_back/pallas_call | solution.py:622
  198.2 0.0 copy-start.1
  198.2 0.0 copy-done
  198.2 1.3 convert_add_fusion
  199.5 0.0 copy-done.1
  199.5 0.1 fusion.1
  199.6 0.1 fusion
  199.7 0.1 convert_element_type.17
  199.7 0.8 fusion.2
  (1 shorter events, 0.0 us)
Async XLA Ops:
  108.5 89.7 %copy-start = (f32[2,4,64,512]{3,2,1,0:T(8,128)S(1)}, f32[2,4,64,512]{3,2,1,0:T(8,128)}, u32[]{:S(2)}) copy-start(f32[2,4,64,512]{3,2,1,0:T(8,128)} %get-tuple-element.43) | copy-start | bytes 3145732
  198.2 1.3 copy-start.1

commit v4 on v3

--- a/solution.py
+++ b/solution.py
@@ -20,6 +20,8 @@
 PARTS = 4
 PART = 128
 ROWS = BLK // 2
+CAP = 15
+TERMS = SLOTS + 3 * CAP
 VMEM_LIMIT = 56 * 1024 * 1024
 
 
@@ -644,30 +646,500 @@
     )(prev, last, terms, rims)
 
 
+def list_kernel(table, wide_ref, at_ref, pos_ref, back_ref, prev_ref, last_ref, most_ref, count):
+    me, z, x, c = place()
+
+    source = lax.rem(lax.div(wide_ref[...], 8), NX)
+    chip = lax.rem(lax.broadcasted_iota(jnp.int32, source.shape, 0), NX)
+    most = jnp.int32(0)
+    for s in range(NX):
+        hits = ((source == s) & (chip != s)).astype(jnp.int32)
+        most = jnp.maximum(most, jnp.max(jnp.sum(hits, axis=1, keepdims=True)))
+    most_ref[0] = most
+
+    @pl.loop(0, NZ * 8)
+    def _(at):
+        last_ref[at] = TERMS
+
+    @pl.loop(0, 3 * CAP)
+    def _(n):
+        at_ref[n] = 0
+        back_ref[n] = 0
+        prev_ref[SLOTS + n] = TERMS
+
+    for r in range(NX):
+        count[r] = 0
+
+    @pl.loop(0, SLOTS)
+    def _(slot):
+        holder, at = block_place(table[(z * NX + x) * SLOTS + slot])
+        pos_ref[slot] = 0
+        prev_ref[slot] = TERMS
+        r = lax.rem(holder - x + NX, NX)
+
+        @pl.when(r == 0)
+        def _():
+            prev_ref[slot] = last_ref[at]
+            last_ref[at] = slot
+
+        @pl.when(r > 0)
+        def _():
+            j = count[r]
+            count[r] = j + 1
+
+            @pl.when(j < CAP)
+            def _():
+                pos_ref[slot] = (r - 1) * CAP + j
+                back_ref[(r - 1) * CAP + j] = slot
+
+    for r in range(1, NX):
+        count[0] = 0
+
+        @pl.loop(0, SLOTS)
+        def _(slot):
+            holder, at = block_place(table[(z * NX + lax.rem(x + r, NX)) * SLOTS + slot])
+
+            @pl.when(holder == x)
+            def _():
+                j = count[0]
+                count[0] = j + 1
+
+                @pl.when(j < CAP)
+                def _():
+                    n = (r - 1) * CAP + j
+                    at_ref[n] = at
+                    prev_ref[SLOTS + n] = last_ref[at]
+                    last_ref[at] = SLOTS + n
+
+
+def make_lists(table):
+    smem = pl.BlockSpec(memory_space=pltpu.SMEM)
+    vmem = pl.BlockSpec(memory_space=pltpu.VMEM)
+    sizes = (3 * CAP, SLOTS, 3 * CAP, TERMS, NZ * 8, 1)
+    return pl.pallas_call(
+        list_kernel,
+        out_shape=tuple(jax.ShapeDtypeStruct((size,), jnp.int32) for size in sizes),
+        in_specs=[smem, vmem],
+        out_specs=(smem,) * 6,
+        scratch_shapes=[pltpu.SMEM((NX,), jnp.int32)],
+        name="make_lists",
+    )(table.reshape(-1), table)
+
+
+def packed_gather_kernel(
+    table, at_list, pos_list, k_ref, v_ref, out_ref, halo_ref,
+    packed, give, pair_sem, halo_send, halo_recv, z_send, z_recv, x_send, x_recv, give_sem, *bufs,
+):
+    ag, landing = bufs[:PARTS], bufs[PARTS:]
+    me, z, x, c = place()
+    other = 1 - c
+    sibling = seq_of(z, x, other)
+    after = lax.rem(me + 1, NSEQ)
+    before = lax.rem(me + NSEQ - 1, NSEQ)
+    zs = (seq_of(z + 1, x, c), seq_of(z - 1, x, c))
+    xs = tuple(seq_of(z, x + r, c) for r in range(1, NX))
+    greet((after, before) + zs + xs)
+
+    def lanes(p):
+        return pl.ds(p * PART, PART)
+
+    def pair_copy(src, p):
+        return remote(
+            src.at[:, :, lanes(p)], ag[p].at[pl.ds(z * 8 + c * 4, 4)],
+            pair_sem.at[0, p], pair_sem.at[1, p], sibling,
+        )
+
+    @pl.when(c == 0)
+    def _():
+        for p in range(PARTS):
+            pair_copy(v_ref, p).start()
+        for p in range(PARTS):
+            ag[p][pl.ds(z * 8, 4)] = k_ref[:, :, p * PART : (p + 1) * PART]
+
+    @pl.when(c == 1)
+    def _():
+        for p in range(PARTS):
+            pair_copy(k_ref, p).start()
+        for p in range(PARTS):
+            ag[p][pl.ds(z * 8 + 4, 4)] = v_ref[:, :, p * PART : (p + 1) * PART]
+
+    def z_piece(p, direction, step, half):
+        origin = lax.rem(z + NZ - (step - 1), NZ) if direction == 0 else lax.rem(z + step - 1, NZ)
+        piece = ag[p].at[pl.ds(origin * 8 + half * 4, 4)]
+        return remote(
+            piece,
+            piece,
+            z_send.at[p, direction, step - 1, half],
+            z_recv.at[p, direction, step - 1, half],
+            zs[direction],
+        )
+
+    def z_start(p):
+        for direction in range(2):
+            z_piece(p, direction, 1, c).start()
+        pair_copy(v_ref, p).wait()
+        for direction in range(2):
+            z_piece(p, direction, 1, other).start()
+
+    def z_step(p, step):
+        for half in range(2):
+            for direction in range(2):
+                if step <= Z_LAST[direction, half]:
+                    z_piece(p, direction, step, half).wait_recv()
+                    if step + 1 <= Z_LAST[direction, half]:
+                        z_piece(p, direction, step + 1, half).start()
+
+    def x_copy(p, r):
+        return remote(
+            packed.at[p, pl.ds((r - 1) * CAP, CAP)],
+            landing[p].at[pl.ds((NX - 1 - r) * CAP, CAP)],
+            x_send.at[p, r - 1],
+            x_recv.at[p, NX - 1 - r],
+            xs[r - 1],
+        )
+
+    def x_start(p):
+        for r in (2, 1, 3):
+            @pl.loop(0, CAP, unroll=3)
+            def _(j):
+                n = (r - 1) * CAP + j
+                packed[p, n] = ag[p][at_list[n]]
+
+            x_copy(p, r).start()
+
+    def chosen(p, slot):
+        holder, at = block_place(table[(z * NX + x) * SLOTS + slot])
+        return jnp.where(holder == x, ag[p][at], landing[p][pos_list[slot]])
+
+    def handed(p):
+        return remote(
+            give.at[p], out_ref.at[c, :, :, lanes(p)], give_sem.at[0, p], give_sem.at[1, p],
+            sibling,
+        )
+
+    def finish(p):
+        for r in range(1, NX):
+            x_copy(p, r).wait_recv()
+        columns = slice(p * PART, (p + 1) * PART)
+
+        @pl.loop(0, REQ, unroll=2)
+        def _(i):
+            give[p, i] = chosen(p, other * (REQ + 2) + i)
+
+        for i in range(2):
+            value = chosen(p, REQ + i)
+            give[p, REQ + i] = value
+            out_ref[c, REQ + i, :, columns] = value
+        handed(p).start()
+
+        @pl.loop(0, REQ, unroll=2)
+        def _(i):
+            out_ref[c, i, :, columns] = chosen(p, c * (REQ + 2) + i)
+
+    halos = []
+    for number, ref in enumerate((k_ref, v_ref)):
+        for side, (row, target) in enumerate(((BLK_DEV - 1, after), (0, before))):
+            halos.append(
+                remote(
+                    ref.at[row], halo_ref.at[number, side], halo_send.at[number, side],
+                    halo_recv.at[number, side], target,
+                )
+            )
+
+    z_start(0)
+    for turn in range(1, 2 * PARTS + 6):
+        for p in range(PARTS):
+            step = turn - 2 * p
+            if step == 0:
+                z_start(p)
+            if 1 <= step <= 4:
+                z_step(p, step)
+            if step == 4:
+                x_start(p)
+            if step == 7:
+                finish(p)
+        if turn == 3:
+            for copy in halos:
+                copy.start()
+
+    for copy in halos:
+        copy.wait()
+    for p in range(PARTS):
+        for (direction, half), last in Z_LAST.items():
+            for step in range(1, last + 1):
+                z_piece(p, direction, step, half).wait_send()
+        for r in range(1, NX):
+            x_copy(p, r).wait_send()
+        handed(p).wait()
+
+
+def packed_gather(table, at_list, pos_list, k, v):
+    features = k.shape[-1]
+    vmem = pl.BlockSpec(memory_space=pltpu.VMEM)
+    smem = pl.BlockSpec(memory_space=pltpu.SMEM)
+    dma = pltpu.SemaphoreType.DMA
+    return pl.pallas_call(
+        packed_gather_kernel,
+        out_shape=(
+            jax.ShapeDtypeStruct((2, REQ + 2, BLK, features), jnp.bfloat16),
+            jax.ShapeDtypeStruct((2, 2, BLK, features), jnp.bfloat16),
+        ),
+        in_specs=[smem, smem, smem, vmem, vmem],
+        out_specs=(vmem, vmem),
+        scratch_shapes=[
+            pltpu.VMEM((PARTS, 3 * CAP, BLK, PART), jnp.bfloat16),
+            pltpu.VMEM((PARTS, REQ + 2, BLK, PART), jnp.bfloat16),
+            dma((2, PARTS)), dma((2, 2)), dma((2, 2)), dma((PARTS, 2, 4, 2)), dma((PARTS, 2, 4, 2)),
+            dma((PARTS, 3)), dma((PARTS, 3)), dma((2, PARTS)),
+        ]
+        + [pltpu.VMEM((NZ * 8, BLK, PART), jnp.bfloat16)] * PARTS
+        + [pltpu.VMEM((3 * CAP, BLK, PART), jnp.bfloat16)] * PARTS,
+        compiler_params=pltpu.CompilerParams(
+            collective_id=2, has_side_effects=True, vmem_limit_bytes=VMEM_LIMIT
+        ),
+        name="packed_gather",
+    )(table, at_list, pos_list, k, v)
+
+
+def packed_back_kernel(
+    back_list, prev, last, term_ref, rim_ref, out_ref, edge_ref,
+    theirs, own, packed, arrived, chain, landed, send_buf, recv_buf, give,
+    pair_sem, rim_send, rim_recv, x_send, x_recv, z_send, z_recv, give_sem,
+):
+    me, z, x, c = place()
+    other = 1 - c
+    sibling = seq_of(z, x, other)
+    after = lax.rem(me + 1, NSEQ)
+    before = lax.rem(me + NSEQ - 1, NSEQ)
+    xs = tuple(seq_of(z, x + r, c) for r in range(1, NX))
+    zs = (seq_of(z + 1, x, c), seq_of(z - 1, x, c))
+    greet((after, before) + zs + xs)
+
+    def lanes(p):
+        return pl.ds(p * PART, PART)
+
+    def pair(p):
+        return remote(
+            term_ref.at[other, :, :, lanes(p)], theirs.at[p], pair_sem.at[0, p],
+            pair_sem.at[1, p], sibling,
+        )
+
+    for p in range(PARTS):
+        pair(p).start()
+
+    def x_copy(p, r):
+        return remote(
+            packed.at[p, pl.ds((r - 1) * CAP, CAP)],
+            arrived.at[p, pl.ds((NX - 1 - r) * CAP, CAP)],
+            x_send.at[p, r - 1],
+            x_recv.at[p, NX - 1 - r],
+            xs[r - 1],
+        )
+
+    def x_start(p):
+        columns = slice(p * PART, (p + 1) * PART)
+
+        @pl.loop(0, REQ, unroll=2)
+        def _(i):
+            own[p, c * (REQ + 2) + i] = term_ref[c, i, :, columns]
+
+        pair(p).wait_recv()
+
+        @pl.loop(0, REQ, unroll=2)
+        def _(i):
+            own[p, other * (REQ + 2) + i] = theirs[p, i]
+
+        for i in range(2):
+            total = term_ref[c, REQ + i, :, columns].astype(jnp.float32) + theirs[
+                p, REQ + i
+            ].astype(jnp.float32)
+            own[p, REQ + i] = total.astype(jnp.bfloat16)
+        for r in (2, 1, 3):
+            @pl.loop(0, CAP, unroll=3)
+            def _(j):
+                n = (r - 1) * CAP + j
+                packed[p, n] = own[p, back_list[n]]
+
+            x_copy(p, r).start()
+
+    chain[TERMS] = jnp.zeros((BLK, PART), jnp.float32)
+
+    def land(p):
+        @pl.loop(0, SLOTS, unroll=2)
+        def _(n):
+            chain[n] = own[p, n].astype(jnp.float32) + chain[prev[n]]
+
+        for r in range(1, NX):
+            x_copy(p, r).wait_recv()
+
+        @pl.loop(0, 3 * CAP, unroll=3)
+        def _(n):
+            chain[SLOTS + n] = arrived[p, n].astype(jnp.float32) + chain[prev[SLOTS + n]]
+
+        @pl.loop(0, NZ * 8, unroll=4)
+        def _(at):
+            landed[p, at] = chain[last[at]]
+
+    def piece(p, direction, distance, half):
+        return remote(
+            send_buf.at[p, direction, distance - 1, half],
+            recv_buf.at[p, direction, distance - 1, half],
+            z_send.at[p, direction, distance - 1, half],
+            z_recv.at[p, direction, distance - 1, half],
+            zs[direction],
+        )
+
+    def z_step(p, distance):
+        for half in range(2):
+            for direction in range(2):
+                if distance > Z_LAST[direction, half]:
+                    continue
+                target = lax.rem(z + (distance if direction == 0 else NZ - distance), NZ)
+                first = target * 8 + half * 4
+                waits = distance < Z_LAST[direction, half]
+                if waits:
+                    piece(p, direction, distance + 1, half).wait_recv()
+                for i in range(BLK_DEV):
+                    total = landed[p, first + i]
+                    if waits:
+                        total += recv_buf[p, direction, distance, half, i].astype(jnp.float32)
+                    send_buf[p, direction, distance - 1, half, i] = total.astype(jnp.bfloat16)
+                piece(p, direction, distance, half).start()
+
+    def handed(p):
+        return remote(
+            give.at[p], out_ref.at[c, :, :, lanes(p)], give_sem.at[0, p], give_sem.at[1, p],
+            sibling,
+        )
+
+    def finish(p):
+        columns = slice(p * PART, (p + 1) * PART)
+        for half in range(2):
+            for direction in range(2):
+                piece(p, direction, 1, half).wait_recv()
+
+        def finished(half, i):
+            total = landed[p, z * 8 + half * 4 + i]
+            for direction in range(2):
+                total += recv_buf[p, direction, 0, half, i].astype(jnp.float32)
+            return total.astype(jnp.bfloat16)
+
+        for i in range(BLK_DEV):
+            give[p, i] = finished(other, i)
+        handed(p).start()
+        for i in range(BLK_DEV):
+            out_ref[c, i, :, columns] = finished(c, i)
+
+    edges = []
+    for number in range(2):
+        for side, target in enumerate((after, before)):
+            edges.append(
+                remote(
+                    rim_ref.at[number, 1 - side], edge_ref.at[number, side],
+                    rim_send.at[number, side], rim_recv.at[number, side], target,
+                )
+            )
+
+    x_start(0)
+    x_start(1)
+    for copy in edges:
+        copy.start()
+    for p in range(PARTS):
+        land(p)
+        if p + 2 < PARTS:
+            x_start(p + 2)
+        z_step(p, 4)
+        if p:
+            z_step(p - 1, 2)
+        z_step(p, 3)
+        if p:
+            z_step(p - 1, 1)
+            finish(p - 1)
+    z_step(PARTS - 1, 2)
+    z_step(PARTS - 1, 1)
+    finish(PARTS - 1)
+
+    for copy in edges:
+        copy.wait()
+    for p in range(PARTS):
+        pair(p).wait_send()
+        for r in range(1, NX):
+            x_copy(p, r).wait_send()
+        for (direction, half), most in Z_LAST.items():
+            for distance in range(1, most + 1):
+                piece(p, direction, distance, half).wait_send()
+        handed(p).wait()
+
+
+def packed_back(back_list, prev, last, terms, rims):
+    features = terms.shape[-1]
+    vmem = pl.BlockSpec(memory_space=pltpu.VMEM)
+    smem = pl.BlockSpec(memory_space=pltpu.SMEM)
+    dma = pltpu.SemaphoreType.DMA
+    ring = pltpu.VMEM((PARTS, 2, 4, 2, BLK_DEV, BLK, PART), jnp.bfloat16)
+    return pl.pallas_call(
+        packed_back_kernel,
+        out_shape=(
+            jax.ShapeDtypeStruct((2, BLK_DEV, BLK, features), jnp.bfloat16),
+            jax.ShapeDtypeStruct((2, 2, BLK, features), jnp.bfloat16),
+        ),
+        in_specs=[smem, smem, smem, vmem, vmem],
+        out_specs=(vmem, vmem),
+        scratch_shapes=[
+            pltpu.VMEM((PARTS, REQ + 2, BLK, PART), jnp.bfloat16),
+            pltpu.VMEM((PARTS, SLOTS, BLK, PART), jnp.bfloat16),
+            pltpu.VMEM((PARTS, 3 * CAP, BLK, PART), jnp.bfloat16),
+            pltpu.VMEM((PARTS, 3 * CAP, BLK, PART), jnp.bfloat16),
+            pltpu.VMEM((TERMS + 1, BLK, PART), jnp.float32),
+            pltpu.VMEM((PARTS, NZ * 8, BLK, PART), jnp.float32),
+            ring, ring,
+            pltpu.VMEM((PARTS, BLK_DEV, BLK, PART), jnp.bfloat16),
+            dma((2, PARTS)), dma((2, 2)), dma((2, 2)), dma((PARTS, 3)), dma((PARTS, 3)),
+            dma((PARTS, 2, 4, 2)), dma((PARTS, 2, 4, 2)), dma((2, PARTS)),
+        ],
+        compiler_params=pltpu.CompilerParams(
+            collective_id=3, has_side_effects=True, vmem_limit_bytes=VMEM_LIMIT
+        ),
+        name="packed_back",
+    )(back_list, prev, last, terms, rims)
+
+
 def per_device(queries, key_rows, value_rows, out_grad, random_blocks, global_blocks):
     row_count, features = queries.shape
     blocks = (BLK_DEV, BLK, features)
     lists = random_blocks.reshape(NZ * NX, NC, REQ)
     shared = jnp.broadcast_to(global_blocks[None], (NZ * NX, 2))
-    table = jnp.concatenate([lists[:, 0], shared, lists[:, 1]], axis=1).reshape(-1)
+    table = jnp.concatenate([lists[:, 0], shared, lists[:, 1]], axis=1)
     k = key_rows.reshape(blocks)
     v = value_rows.reshape(blocks)
-    prev, last = plan(table)
-    slots, halo = gather(table, k, v)
-    attended, query_grad, wacc, terms, rims = attend(
-        queries.reshape(blocks), out_grad.reshape(blocks), k, v, halo, slots
-    )
-    total, edges = send_back(prev, last, terms, rims)
+    q = queries.reshape(blocks)
+    g = out_grad.reshape(blocks)
+    at_list, pos_list, back_list, chain_prev, chain_last, most = make_lists(table)
+
+    def packed():
+        slots, halo = packed_gather(table.reshape(-1), at_list, pos_list, k, v)
+        attended, query_grad, wacc, terms, rims = attend(q, g, k, v, halo, slots)
+        total, edges = packed_back(back_list, chain_prev, chain_last, terms, rims)
+        return attended, query_grad, *joined(wacc, total, edges)
+
+    def unpacked():
+        flat = table.reshape(-1)
+        prev, last = plan(flat)
+        slots, halo = gather(flat, k, v)
+        attended, query_grad, wacc, terms, rims = attend(q, g, k, v, halo, slots)
+        total, edges = send_back(prev, last, terms, rims)
+        return attended, query_grad, *joined(wacc, total, edges)
+
+    results = lax.cond(most[0] <= CAP, packed, unpacked)
+    return tuple(result.reshape(row_count, features) for result in results)
+
+
+def joined(wacc, total, edges):
     gradient = wacc + total.astype(jnp.float32)
     gradient = gradient.at[:, 0].add(edges[:, 0].astype(jnp.float32))
     gradient = gradient.at[:, BLK_DEV - 1].add(edges[:, 1].astype(jnp.float32))
     gradient = gradient.astype(jnp.bfloat16)
-    return (
-        attended.reshape(row_count, features),
-        query_grad.reshape(row_count, features),
-        gradient[0].reshape(row_count, features),
-        gradient[1].reshape(row_count, features),
-    )
+    return gradient[0], gradient[1]
 
 
 def solution(mesh):

time: 201 us -> 177 us (0.88)
  Pallas kernels: 195 us -> 169 us
    pallas_call x3, Pallas kernels: 187 us -> 160 us  [the longest x1 78.5 us: packed_back(): pl.pallas_call(packed_back_kernel, out_shape=(jax.ShapeDtypeStruct((2, BL...]
where the time goes in v4:
time: 177 us; the launch traced here: 176 us
  Pallas kernels  169 us (95%)
  local copies, waits for them, and re-layouts  4.04 us (2%)
    pallas_call x1, Pallas kernels, packed_back(): pl.pallas_call(packed_back_kernel, out_shape=(jax.ShapeDtypeStruct((2, BL...  78.5 us
    pallas_call x1, Pallas kernels, packed_gather(): pl.pallas_call(packed_gather_kernel, out_shape=(jax.ShapeDtypeStruct((2,...  77.1 us
    pallas_call x1, Pallas kernels, attend(): pl.pallas_call(attend_kernel, out_shape=(own, own, jax.ShapeDtypeStruct((...  8.27 us
    pallas_call x1, Pallas kernels, make_lists(): pl.pallas_call(list_kernel, out_shape=tuple((jax.ShapeDtypeStruct((size,)...  4.67 us

profile of v4, /device:TPU:1, one launch (start us, length us, event | category | flops | bytes accessed | tf_op | source)
XLA Modules:
  0.0 175.8 jit_solution(5317245929462536185)
XLA Ops:
  0.6 0.7 pad.9.clone
  1.4 0.8 copy.10
  2.2 0.1 reshape.197
  2.3 0.1 pad_add_fusion.wide_ref
  2.4 0.7 reshape.198.table
  3.1 4.7 %make_lists.1 = (s32[45]{0:T(128)S(1)}, s32[26]{0:T(128)S(1)}, s32[45]{0:T(128)S(1)}, s32[71]{0:T(128)S(1)}, s32[64]{0:T(128)S(1)}, /*index=5*/s32[1]{0:T(128)}) custom-call(s32[832]{0:T(1024)} %reshape.198.table, s32[32,26]{1,0:T(8,128)S(1)} %pad_add_fusion.wide_ref), custom_call_target="tpu_custom_call" | custom-call | tf_op jit(solution)/shard_map/make_lists/pallas_call | solution.py:719
  8.4 166.4 %conditional.1 = (bf16[4,64,512]{2,1,0:T(8,128)(2,1)S(1)}, bf16[4,64,512]{2,1,0:T(8,128)(2,1)S(1)}, bf16[256,512]{1,0:T(8,128)(2,1)S(1)}, bf16[256,512]{1,0:T(8,128)(2,1)S(1)}) conditional(s32[]{:T(128)} %bitcast.6, (s32[32,26]{1,0:T(8,128)S(1)}, bf16[4,64,512]{2,1,0:T(8,128)(2,1)}, bf16[4,64,512]{2,1,0:T(8,128)(2,1)}, bf16[4,64,512]{2,1,0:T(8,128)(2,1)}, ...), branch_computations={%region_0.1_spmd, %region_1.2_spmd} | conditional | flops 1048576 | bytes 11803224 | solution.py:1133
  8.4 0.7 reshape.186.table
  9.1 77.1 %packed_gather.1 = (bf16[2,14,64,512]{3,2,1,0:T(8,128)(2,1)}, bf16[2,2,64,512]{3,2,1,0:T(8,128)(2,1)}) custom-call(s32[832]{0:T(1024)} %reshape.186.table, s32[45]{0:T(128)S(1)} %get-tuple-element.101.at_list, s32[26]{0:T(128)S(1)} %get-tuple-element.102.pos_list, bf16[4,64,512]{2,1,0:T(8,128)(2,1)} %get-tuple-element.98.k_ref, ...), custom_call_target="tpu_custom_call" | custom-call | tf_op jit(solution)/shard_map/cond/branch_1_fun/packed_gather/pallas_call | solution.py:881
  86.3 8.3 %attend_blocks.3 = (bf16[4,64,512]{2,1,0:T(8,128)(2,1)S(1)}, bf16[4,64,512]{2,1,0:T(8,128)(2,1)S(1)}, f32[2,4,64,512]{3,2,1,0:T(8,128)}, bf16[2,14,64,512]{3,2,1,0:T(8,128)(2,1)}, bf16[2,2,64,512]{3,2,1,0:T(8,128)(2,1)}) custom-call(bf16[4,64,512]{2,1,0:T(8,128)(2,1)} %get-tuple-element.96.q_ref, bf16[4,64,512]{2,1,0:T(8,128)(2,1)} %get-tuple-element.97.g_ref, ...), custom_call_target="tpu_custom_call" | custom-call | tf_op jit(solution)/shard_map/cond/branch_1_fun/attend_blocks/pallas_call | solution.py:379
  94.5 0.0 copy-start.1
  94.5 78.5 %packed_back.1 = (bf16[2,4,64,512]{3,2,1,0:T(8,128)(2,1)}, bf16[2,2,64,512]{3,2,1,0:T(8,128)(2,1)}) custom-call(s32[45]{0:T(128)S(1)} %get-tuple-element.108.back_list, s32[71]{0:T(128)S(1)} %get-tuple-element.109.prev, s32[64]{0:T(128)S(1)} %get-tuple-element.110.last, bf16[2,14,64,512]{3,2,1,0:T(8,128)(2,1)} %get-tuple-element.111.term_ref, ...), custom_call_target="tpu_custom_call" | custom-call | tf_op jit(solution)/shard_map/cond/branch_1_fun/packed_back/pallas_call | solution.py:1080
  173.1 0.0 copy-start.3
  173.1 0.0 copy-done.1
  173.1 1.3 convert_add_fusion.1
  174.4 0.0 copy-done.3
  174.4 0.1 fusion.3
  174.4 0.1 fusion.2
  174.5 0.1 convert_element_type.31
  174.8 0.0 copy-start.4
  174.9 0.0 copy-start.5
  174.9 0.0 copy-start.6
  174.9 0.0 copy-start.7
  174.9 0.7 copy-done.4
  175.5 0.1 copy-done.5
  175.6 0.1 copy-done.6
  175.7 0.1 copy-done.7
  (2 shorter events, 0.1 us)
Async XLA Ops:
  94.5 78.5 %copy-start.1 = (f32[2,4,64,512]{3,2,1,0:T(8,128)S(1)}, f32[2,4,64,512]{3,2,1,0:T(8,128)}, u32[]{:S(2)}) copy-start(f32[2,4,64,512]{3,2,1,0:T(8,128)} %get-tuple-element.107) | copy-start | bytes 3145732 | tf_op jit(solution)/shard_map/cond
  173.1 1.3 copy-start.3
  174.8 0.7 copy-start.4
  174.9 0.8 copy-start.5
  174.9 0.9 copy-start.6
  174.9 0.9 copy-start.7

commit v5 on v4

--- a/solution.py
+++ b/solution.py
@@ -726,9 +726,14 @@
     )(table.reshape(-1), table)
 
 
-def packed_gather_kernel(
-    table, at_list, pos_list, k_ref, v_ref, out_ref, halo_ref,
-    packed, give, pair_sem, halo_send, halo_recv, z_send, z_recv, x_send, x_recv, give_sem, *bufs,
+def layer_kernel(
+    table, at_list, pos_list, back_list, prev, last, q_ref, g_ref, k_ref, v_ref,
+    att_ref, qg_ref, wacc_ref, out_ref, edge_ref,
+    packed, give, kv, halo, wide, window, shared, terms, rim,
+    theirs, own, back_packed, arrived, chain, landed, send_buf, recv_buf, give_back,
+    pair_sem, halo_send, halo_recv, z_send, z_recv, x_send, x_recv, give_sem,
+    back_pair, rim_send, rim_recv, bx_send, bx_recv, bz_send, bz_recv, back_give,
+    *bufs,
 ):
     ag, landing = bufs[:PARTS], bufs[PARTS:]
     me, z, x, c = place()
@@ -743,6 +748,9 @@
     def lanes(p):
         return pl.ds(p * PART, PART)
 
+    def columns(p):
+        return slice(p * PART, (p + 1) * PART)
+
     def pair_copy(src, p):
         return remote(
             src.at[:, :, lanes(p)], ag[p].at[pl.ds(z * 8 + c * 4, 4)],
@@ -754,14 +762,14 @@
         for p in range(PARTS):
             pair_copy(v_ref, p).start()
         for p in range(PARTS):
-            ag[p][pl.ds(z * 8, 4)] = k_ref[:, :, p * PART : (p + 1) * PART]
+            ag[p][pl.ds(z * 8, 4)] = k_ref[:, :, columns(p)]
 
     @pl.when(c == 1)
     def _():
         for p in range(PARTS):
             pair_copy(k_ref, p).start()
         for p in range(PARTS):
-            ag[p][pl.ds(z * 8 + 4, 4)] = v_ref[:, :, p * PART : (p + 1) * PART]
+            ag[p][pl.ds(z * 8 + 4, 4)] = v_ref[:, :, columns(p)]
 
     def z_piece(p, direction, step, half):
         origin = lax.rem(z + NZ - (step - 1), NZ) if direction == 0 else lax.rem(z + step - 1, NZ)
@@ -812,15 +820,11 @@
         return jnp.where(holder == x, ag[p][at], landing[p][pos_list[slot]])
 
     def handed(p):
-        return remote(
-            give.at[p], out_ref.at[c, :, :, lanes(p)], give_sem.at[0, p], give_sem.at[1, p],
-            sibling,
-        )
-
-    def finish(p):
+        return remote(give.at[p], kv.at[p, c], give_sem.at[0, p], give_sem.at[1, p], sibling)
+
+    def x_finish(p):
         for r in range(1, NX):
             x_copy(p, r).wait_recv()
-        columns = slice(p * PART, (p + 1) * PART)
 
         @pl.loop(0, REQ, unroll=2)
         def _(i):
@@ -829,119 +833,100 @@
         for i in range(2):
             value = chosen(p, REQ + i)
             give[p, REQ + i] = value
-            out_ref[c, REQ + i, :, columns] = value
+            kv[p, c, REQ + i] = value
         handed(p).start()
 
         @pl.loop(0, REQ, unroll=2)
         def _(i):
-            out_ref[c, i, :, columns] = chosen(p, c * (REQ + 2) + i)
+            kv[p, c, i] = chosen(p, c * (REQ + 2) + i)
 
     halos = []
     for number, ref in enumerate((k_ref, v_ref)):
         for side, (row, target) in enumerate(((BLK_DEV - 1, after), (0, before))):
             halos.append(
                 remote(
-                    ref.at[row], halo_ref.at[number, side], halo_send.at[number, side],
+                    ref.at[row], halo.at[number, side], halo_send.at[number, side],
                     halo_recv.at[number, side], target,
                 )
             )
 
-    z_start(0)
-    for turn in range(1, 2 * PARTS + 6):
-        for p in range(PARTS):
-            step = turn - 2 * p
-            if step == 0:
-                z_start(p)
-            if 1 <= step <= 4:
-                z_step(p, step)
-            if step == 4:
-                x_start(p)
-            if step == 7:
-                finish(p)
-        if turn == 3:
-            for copy in halos:
-                copy.start()
-
-    for copy in halos:
-        copy.wait()
-    for p in range(PARTS):
-        for (direction, half), last in Z_LAST.items():
-            for step in range(1, last + 1):
-                z_piece(p, direction, step, half).wait_send()
-        for r in range(1, NX):
-            x_copy(p, r).wait_send()
+    scale = 1.0 / math.sqrt(HEAD_DIM)
+    entry = lax.broadcasted_iota(jnp.int32, (BLK, 8 * BLK), 1) // BLK
+
+    def attend_part(p):
         handed(p).wait()
-
-
-def packed_gather(table, at_list, pos_list, k, v):
-    features = k.shape[-1]
-    vmem = pl.BlockSpec(memory_space=pltpu.VMEM)
-    smem = pl.BlockSpec(memory_space=pltpu.SMEM)
-    dma = pltpu.SemaphoreType.DMA
-    return pl.pallas_call(
-        packed_gather_kernel,
-        out_shape=(
-            jax.ShapeDtypeStruct((2, REQ + 2, BLK, features), jnp.bfloat16),
-            jax.ShapeDtypeStruct((2, 2, BLK, features), jnp.bfloat16),
-        ),
-        in_specs=[smem, smem, smem, vmem, vmem],
-        out_specs=(vmem, vmem),
-        scratch_shapes=[
-            pltpu.VMEM((PARTS, 3 * CAP, BLK, PART), jnp.bfloat16),
-            pltpu.VMEM((PARTS, REQ + 2, BLK, PART), jnp.bfloat16),
-            dma((2, PARTS)), dma((2, 2)), dma((2, 2)), dma((PARTS, 2, 4, 2)), dma((PARTS, 2, 4, 2)),
-            dma((PARTS, 3)), dma((PARTS, 3)), dma((2, PARTS)),
-        ]
-        + [pltpu.VMEM((NZ * 8, BLK, PART), jnp.bfloat16)] * PARTS
-        + [pltpu.VMEM((3 * CAP, BLK, PART), jnp.bfloat16)] * PARTS,
-        compiler_params=pltpu.CompilerParams(
-            collective_id=2, has_side_effects=True, vmem_limit_bytes=VMEM_LIMIT
-        ),
-        name="packed_gather",
-    )(table, at_list, pos_list, k, v)
-
-
-def packed_back_kernel(
-    back_list, prev, last, term_ref, rim_ref, out_ref, edge_ref,
-    theirs, own, packed, arrived, chain, landed, send_buf, recv_buf, give,
-    pair_sem, rim_send, rim_recv, x_send, x_recv, z_send, z_recv, give_sem,
-):
-    me, z, x, c = place()
-    other = 1 - c
-    sibling = seq_of(z, x, other)
-    after = lax.rem(me + 1, NSEQ)
-    before = lax.rem(me + NSEQ - 1, NSEQ)
-    xs = tuple(seq_of(z, x + r, c) for r in range(1, NX))
-    zs = (seq_of(z + 1, x, c), seq_of(z - 1, x, c))
-    greet((after, before) + zs + xs)
-
-    def lanes(p):
-        return pl.ds(p * PART, PART)
+        for number, ref in enumerate((k_ref, v_ref)):
+            wide[number, 0] = halo[number, 0, :, columns(p)]
+            wide[number, BLK_DEV + 1] = halo[number, 1, :, columns(p)]
+            for i in range(BLK_DEV):
+                wide[number, i + 1] = ref[i, :, columns(p)]
+        window[...] = jnp.zeros_like(window)
+        shared[...] = jnp.zeros_like(shared)
+
+        @pl.loop(0, BLK_DEV)
+        def _(b):
+            def listed(number):
+                return jnp.concatenate(
+                    [wide[number, b + i] for i in range(3)]
+                    + [kv[p, number, REQ + i] for i in range(2)]
+                    + [kv[p, number, 3 * b + i] for i in range(3)],
+                    axis=0,
+                )
+
+            keys = listed(0)
+            values = listed(1)
+            query = q_ref[b, :, columns(p)]
+            grad = g_ref[b, :, columns(p)]
+            low = jnp.where(me * BLK_DEV + b == 0, 0, -1)
+            high = jnp.where(me * BLK_DEV + b == NSEQ * BLK_DEV - 1, 2, -1)
+            scores = nt(query, keys) * scale
+            scores = jnp.where((entry == low) | (entry == high), -jnp.inf, scores)
+            row_max = jnp.max(scores, axis=1, keepdims=True)
+            raw = jnp.exp(scores - row_max)
+            weights = raw * (1.0 / jnp.sum(raw, axis=1, keepdims=True))
+            weights_b = weights.astype(jnp.bfloat16)
+            weight_grads = nt(grad, values)
+            row_dot = jnp.sum(weights_b.astype(jnp.float32) * weight_grads, axis=1, keepdims=True)
+            score_grads = (weights * (weight_grads - row_dot) * scale).astype(jnp.bfloat16)
+            att_ref[b, :, columns(p)] = nn(weights_b, values).astype(jnp.bfloat16)
+            qg_ref[b, :, columns(p)] = nn(score_grads, keys).astype(jnp.bfloat16)
+            for number, made in enumerate((tn(score_grads, query), tn(weights_b, grad))):
+                for i in range(3):
+                    window[number, b + i] += made[i * BLK : (i + 1) * BLK]
+                for i in range(2):
+                    shared[number, i] += made[(3 + i) * BLK : (4 + i) * BLK]
+                for i in range(3):
+                    terms[p, number, 3 * b + i] = made[(5 + i) * BLK : (6 + i) * BLK].astype(
+                        jnp.bfloat16
+                    )
+
+        for number in range(2):
+            for i in range(2):
+                terms[p, number, REQ + i] = shared[number, i].astype(jnp.bfloat16)
+            rim[number, 0, :, columns(p)] = window[number, 0].astype(jnp.bfloat16)
+            rim[number, 1, :, columns(p)] = window[number, BLK_DEV + 1].astype(jnp.bfloat16)
+            for i in range(BLK_DEV):
+                wacc_ref[number, i, :, columns(p)] = window[number, i + 1]
+        pair(p).start()
 
     def pair(p):
         return remote(
-            term_ref.at[other, :, :, lanes(p)], theirs.at[p], pair_sem.at[0, p],
-            pair_sem.at[1, p], sibling,
-        )
-
-    for p in range(PARTS):
-        pair(p).start()
-
-    def x_copy(p, r):
-        return remote(
-            packed.at[p, pl.ds((r - 1) * CAP, CAP)],
+            terms.at[p, other], theirs.at[p], back_pair.at[0, p], back_pair.at[1, p], sibling
+        )
+
+    def bx_copy(p, r):
+        return remote(
+            back_packed.at[p, pl.ds((r - 1) * CAP, CAP)],
             arrived.at[p, pl.ds((NX - 1 - r) * CAP, CAP)],
-            x_send.at[p, r - 1],
-            x_recv.at[p, NX - 1 - r],
+            bx_send.at[p, r - 1],
+            bx_recv.at[p, NX - 1 - r],
             xs[r - 1],
         )
 
-    def x_start(p):
-        columns = slice(p * PART, (p + 1) * PART)
-
+    def bx_start(p):
         @pl.loop(0, REQ, unroll=2)
         def _(i):
-            own[p, c * (REQ + 2) + i] = term_ref[c, i, :, columns]
+            own[p, c * (REQ + 2) + i] = terms[p, c, i]
 
         pair(p).wait_recv()
 
@@ -950,17 +935,17 @@
             own[p, other * (REQ + 2) + i] = theirs[p, i]
 
         for i in range(2):
-            total = term_ref[c, REQ + i, :, columns].astype(jnp.float32) + theirs[
-                p, REQ + i
-            ].astype(jnp.float32)
+            total = terms[p, c, REQ + i].astype(jnp.float32) + theirs[p, REQ + i].astype(
+                jnp.float32
+            )
             own[p, REQ + i] = total.astype(jnp.bfloat16)
         for r in (2, 1, 3):
             @pl.loop(0, CAP, unroll=3)
             def _(j):
                 n = (r - 1) * CAP + j
-                packed[p, n] = own[p, back_list[n]]
-
-            x_copy(p, r).start()
+                back_packed[p, n] = own[p, back_list[n]]
+
+            bx_copy(p, r).start()
 
     chain[TERMS] = jnp.zeros((BLK, PART), jnp.float32)
 
@@ -970,7 +955,7 @@
             chain[n] = own[p, n].astype(jnp.float32) + chain[prev[n]]
 
         for r in range(1, NX):
-            x_copy(p, r).wait_recv()
+            bx_copy(p, r).wait_recv()
 
         @pl.loop(0, 3 * CAP, unroll=3)
         def _(n):
@@ -984,12 +969,12 @@
         return remote(
             send_buf.at[p, direction, distance - 1, half],
             recv_buf.at[p, direction, distance - 1, half],
-            z_send.at[p, direction, distance - 1, half],
-            z_recv.at[p, direction, distance - 1, half],
+            bz_send.at[p, direction, distance - 1, half],
+            bz_recv.at[p, direction, distance - 1, half],
             zs[direction],
         )
 
-    def z_step(p, distance):
+    def bz_step(p, distance):
         for half in range(2):
             for direction in range(2):
                 if distance > Z_LAST[direction, half]:
@@ -1006,14 +991,13 @@
                     send_buf[p, direction, distance - 1, half, i] = total.astype(jnp.bfloat16)
                 piece(p, direction, distance, half).start()
 
-    def handed(p):
-        return remote(
-            give.at[p], out_ref.at[c, :, :, lanes(p)], give_sem.at[0, p], give_sem.at[1, p],
+    def handed_back(p):
+        return remote(
+            give_back.at[p], out_ref.at[c, :, :, lanes(p)], back_give.at[0, p], back_give.at[1, p],
             sibling,
         )
 
-    def finish(p):
-        columns = slice(p * PART, (p + 1) * PART)
+    def bz_finish(p):
         for half in range(2):
             for direction in range(2):
                 piece(p, direction, 1, half).wait_recv()
@@ -1025,83 +1009,110 @@
             return total.astype(jnp.bfloat16)
 
         for i in range(BLK_DEV):
-            give[p, i] = finished(other, i)
-        handed(p).start()
+            give_back[p, i] = finished(other, i)
+        handed_back(p).start()
         for i in range(BLK_DEV):
-            out_ref[c, i, :, columns] = finished(c, i)
+            out_ref[c, i, :, columns(p)] = finished(c, i)
 
     edges = []
     for number in range(2):
         for side, target in enumerate((after, before)):
             edges.append(
                 remote(
-                    rim_ref.at[number, 1 - side], edge_ref.at[number, side],
+                    rim.at[number, 1 - side], edge_ref.at[number, side],
                     rim_send.at[number, side], rim_recv.at[number, side], target,
                 )
             )
 
-    x_start(0)
-    x_start(1)
-    for copy in edges:
-        copy.start()
-    for p in range(PARTS):
-        land(p)
-        if p + 2 < PARTS:
-            x_start(p + 2)
-        z_step(p, 4)
-        if p:
-            z_step(p - 1, 2)
-        z_step(p, 3)
-        if p:
-            z_step(p - 1, 1)
-            finish(p - 1)
-    z_step(PARTS - 1, 2)
-    z_step(PARTS - 1, 1)
-    finish(PARTS - 1)
+    def turn_of(p, turn):
+        step = turn - 2 * p
+        if step == 0:
+            z_start(p)
+        if 1 <= step <= 4:
+            z_step(p, step)
+        if step == 4:
+            x_start(p)
+        if step == 7:
+            x_finish(p)
+        if step == 8:
+            if p == 0:
+                for copy in halos:
+                    copy.wait()
+            attend_part(p)
+            if p == PARTS - 1:
+                for copy in edges:
+                    copy.start()
+            bx_start(p)
+        if step == 12:
+            land(p)
+        if 12 <= step <= 15:
+            bz_step(p, 16 - step)
+        if step == 16:
+            bz_finish(p)
+
+    for turn in range(2 * PARTS + 15):
+        for p in range(PARTS):
+            turn_of(p, turn)
+        if turn == 3:
+            for copy in halos:
+                copy.start()
 
     for copy in edges:
         copy.wait()
     for p in range(PARTS):
-        pair(p).wait_send()
+        for (direction, half), most in Z_LAST.items():
+            for step in range(1, most + 1):
+                z_piece(p, direction, step, half).wait_send()
+                piece(p, direction, step, half).wait_send()
         for r in range(1, NX):
             x_copy(p, r).wait_send()
-        for (direction, half), most in Z_LAST.items():
-            for distance in range(1, most + 1):
-                piece(p, direction, distance, half).wait_send()
-        handed(p).wait()
-
-
-def packed_back(back_list, prev, last, terms, rims):
-    features = terms.shape[-1]
+            bx_copy(p, r).wait_send()
+        pair(p).wait_send()
+        handed_back(p).wait()
+
+
+def layer(table, lists, q, g, k, v):
+    features = k.shape[-1]
     vmem = pl.BlockSpec(memory_space=pltpu.VMEM)
     smem = pl.BlockSpec(memory_space=pltpu.SMEM)
     dma = pltpu.SemaphoreType.DMA
-    ring = pltpu.VMEM((PARTS, 2, 4, 2, BLK_DEV, BLK, PART), jnp.bfloat16)
+    bf16, f32 = jnp.bfloat16, jnp.float32
+
+    def tiles(*lead, dtype=bf16, width=PART):
+        return pltpu.VMEM((*lead, BLK, width), dtype)
+
+    ring = tiles(PARTS, 2, 4, 2, BLK_DEV)
     return pl.pallas_call(
-        packed_back_kernel,
+        layer_kernel,
         out_shape=(
-            jax.ShapeDtypeStruct((2, BLK_DEV, BLK, features), jnp.bfloat16),
-            jax.ShapeDtypeStruct((2, 2, BLK, features), jnp.bfloat16),
+            jax.ShapeDtypeStruct((BLK_DEV, BLK, features), bf16),
+            jax.ShapeDtypeStruct((BLK_DEV, BLK, features), bf16),
+            jax.ShapeDtypeStruct((2, BLK_DEV, BLK, features), f32),
+            jax.ShapeDtypeStruct((2, BLK_DEV, BLK, features), bf16),
+            jax.ShapeDtypeStruct((2, 2, BLK, features), bf16),
         ),
-        in_specs=[smem, smem, smem, vmem, vmem],
-        out_specs=(vmem, vmem),
+        in_specs=[smem] * 6 + [vmem] * 4,
+        out_specs=(vmem,) * 5,
         scratch_shapes=[
-            pltpu.VMEM((PARTS, REQ + 2, BLK, PART), jnp.bfloat16),
-            pltpu.VMEM((PARTS, SLOTS, BLK, PART), jnp.bfloat16),
-            pltpu.VMEM((PARTS, 3 * CAP, BLK, PART), jnp.bfloat16),
-            pltpu.VMEM((PARTS, 3 * CAP, BLK, PART), jnp.bfloat16),
-            pltpu.VMEM((TERMS + 1, BLK, PART), jnp.float32),
-            pltpu.VMEM((PARTS, NZ * 8, BLK, PART), jnp.float32),
-            ring, ring,
-            pltpu.VMEM((PARTS, BLK_DEV, BLK, PART), jnp.bfloat16),
+            tiles(PARTS, 3 * CAP), tiles(PARTS, REQ + 2), tiles(PARTS, 2, REQ + 2),
+            tiles(2, 2, width=features), tiles(2, BLK_DEV + 2),
+            tiles(2, BLK_DEV + 2, dtype=f32), tiles(2, 2, dtype=f32),
+            tiles(PARTS, 2, REQ + 2), tiles(2, 2, width=features),
+            tiles(PARTS, REQ + 2), tiles(PARTS, SLOTS), tiles(PARTS, 3 * CAP),
+            tiles(PARTS, 3 * CAP), tiles(TERMS + 1, dtype=f32),
+            tiles(PARTS, NZ * 8, dtype=f32), ring, ring, tiles(PARTS, BLK_DEV),
+            dma((2, PARTS)), dma((2, 2)), dma((2, 2)), dma((PARTS, 2, 4, 2)), dma((PARTS, 2, 4, 2)),
+            dma((PARTS, 3)), dma((PARTS, 3)), dma((2, PARTS)),
             dma((2, PARTS)), dma((2, 2)), dma((2, 2)), dma((PARTS, 3)), dma((PARTS, 3)),
             dma((PARTS, 2, 4, 2)), dma((PARTS, 2, 4, 2)), dma((2, PARTS)),
-        ],
+        ]
+        + [tiles(NZ * 8)] * PARTS
+        + [tiles(3 * CAP)] * PARTS,
         compiler_params=pltpu.CompilerParams(
-            collective_id=3, has_side_effects=True, vmem_limit_bytes=VMEM_LIMIT
+            collective_id=2, has_side_effects=True, vmem_limit_bytes=VMEM_LIMIT
         ),
-        name="packed_back",
-    )(back_list, prev, last, terms, rims)
+        name="layer",
+    )(table, *lists, q, g, k, v)
 
 
 def per_device(queries, key_rows, value_rows, out_grad, random_blocks, global_blocks):
@@ -1114,13 +1125,11 @@
     v = value_rows.reshape(blocks)
     q = queries.reshape(blocks)
     g = out_grad.reshape(blocks)
-    at_list, pos_list, back_list, chain_prev, chain_last, most = make_lists(table)
+    *packed_lists, most = make_lists(table)
 
     def packed():
-        slots, halo = packed_gather(table.reshape(-1), at_list, pos_list, k, v)
-        attended, query_grad, wacc, terms, rims = attend(q, g, k, v, halo, slots)
-        total, edges = packed_back(back_list, chain_prev, chain_last, terms, rims)
-        return attended, query_grad, *joined(wacc, total, edges)
+        attended, query_grad, *parts = layer(table.reshape(-1), packed_lists, q, g, k, v)
+        return attended, query_grad, *joined(*parts)
 
     def unpacked():
         flat = table.reshape(-1)

time: 177 us -> 160 us (0.904)
  Pallas kernels: 169 us -> 151 us
    pallas_call x3 -> x1, Pallas kernels: 164 us -> 147 us  [layer(): pl.pallas_call(layer_kernel, out_shape=(jax.ShapeDtypeStruct((BLK_DEV, BL...]
where the time goes in v5:
time: 160 us; the launch traced here: 159 us
  Pallas kernels  151 us (94%)
  local copies, waits for them, and re-layouts  4.57 us (3%)
  other arithmetic  1.85 us (1%)
    pallas_call x1, Pallas kernels, layer(): pl.pallas_call(layer_kernel, out_shape=(jax.ShapeDtypeStruct((BLK_DEV, BL...  147 us
    pallas_call x1, Pallas kernels, make_lists(): pl.pallas_call(list_kernel, out_shape=tuple((jax.ShapeDtypeStruct((size,)...  4.67 us

profile of v5, /device:TPU:1, one launch (start us, length us, event | category | flops | bytes accessed | tf_op | source)
XLA Modules:
  0.0 159.4 jit_solution(7363819872256937123)
XLA Ops:
  0.6 0.7 pad.9.clone
  1.4 0.8 copy.10
  2.2 0.1 reshape.197
  2.3 0.1 pad_add_fusion.wide_ref
  2.4 0.7 reshape.198.table
  3.1 4.7 %make_lists.1 = (s32[45]{0:T(128)S(1)}, s32[26]{0:T(128)S(1)}, s32[45]{0:T(128)S(1)}, s32[71]{0:T(128)S(1)}, s32[64]{0:T(128)S(1)}, /*index=5*/s32[1]{0:T(128)}) custom-call(s32[832]{0:T(1024)} %reshape.198.table, s32[32,26]{1,0:T(8,128)S(1)} %pad_add_fusion.wide_ref), custom_call_target="tpu_custom_call" | custom-call | tf_op jit(solution)/shard_map/make_lists/pallas_call | solution.py:719
  8.4 149.4 %conditional.1 = (bf16[4,64,512]{2,1,0:T(8,128)(2,1)S(1)}, bf16[4,64,512]{2,1,0:T(8,128)(2,1)S(1)}, bf16[256,512]{1,0:T(8,128)(2,1)S(1)}, bf16[256,512]{1,0:T(8,128)(2,1)S(1)}) conditional(s32[]{:T(128)} %bitcast.6, (s32[32,26]{1,0:T(8,128)S(1)}, bf16[4,64,512]{2,1,0:T(8,128)(2,1)}, bf16[4,64,512]{2,1,0:T(8,128)(2,1)}, bf16[4,64,512]{2,1,0:T(8,128)(2,1)}, ...), branch_computations={%region_0.1_spmd, %region_1.2_spmd} | conditional | flops 1048576 | bytes 11803224 | solution.py:1142
  8.4 0.7 reshape.186.table
  9.1 146.6 %layer.1 = (bf16[4,64,512]{2,1,0:T(8,128)(2,1)S(1)}, bf16[4,64,512]{2,1,0:T(8,128)(2,1)S(1)}, f32[2,4,64,512]{3,2,1,0:T(8,128)}, bf16[2,4,64,512]{3,2,1,0:T(8,128)(2,1)}, bf16[2,2,64,512]{3,2,1,0:T(8,128)(2,1)}) custom-call(s32[832]{0:T(1024)} %reshape.186.table, s32[45]{0:T(128)S(1)} %get-tuple-element.97.at_list, s32[26]{0:T(128)S(1)} %get-tuple-element.98.pos_list, ...), custom_call_target="tpu_custom_call" | custom-call | tf_op jit(solution)/shard_map/cond/branch_1_fun/layer/pallas_call | solution.py:1085
  155.8 0.0 copy-start.2
  155.8 1.6 convert_add_fusion.1
  157.4 0.0 copy-done.2
  157.4 0.1 fusion.3
  157.5 0.1 fusion.2
  157.5 0.1 convert_element_type.31
  157.9 0.0 copy-start.3
  157.9 0.0 copy-start.4
  157.9 0.8 copy.29
  158.7 0.7 copy.30
  159.4 0.0 copy-done.3
  159.4 0.0 copy-done.4
  (2 shorter events, 0.1 us)
Async XLA Ops:
  155.8 1.6 %copy-start.2 = (bf16[2,2,64,512]{3,2,1,0:T(8,128)(2,1)S(1)}, bf16[2,2,64,512]{3,2,1,0:T(8,128)(2,1)}, u32[]{:S(2)}) copy-start(bf16[2,2,64,512]{3,2,1,0:T(8,128)(2,1)} %get-tuple-element.110) | copy-start | bytes 786436 | tf_op jit(solution)/shard_map/cond
  157.9 1.5 copy-start.3
  157.9 1.5 copy-start.4

commit v6 on v5

--- a/solution.py
+++ b/solution.py
@@ -1,3 +1,4 @@
+import functools
 import math
 
 import jax
@@ -646,22 +647,26 @@
     )(prev, last, terms, rims)
 
 
-def list_kernel(table, wide_ref, at_ref, pos_ref, back_ref, prev_ref, last_ref, most_ref, count):
+def list_kernel(
+    pairs, shared, wide_ref, at_ref, code_ref, back_ref, prev_ref, last_ref, most_ref, count
+):
     me, z, x, c = place()
 
     source = lax.rem(lax.div(wide_ref[...], 8), NX)
-    chip = lax.rem(lax.broadcasted_iota(jnp.int32, source.shape, 0), NX)
-    most = jnp.int32(0)
+    chip = lax.rem(lax.broadcasted_iota(jnp.int32, (NZ * NX, 1), 0), NX)
+    holders = [block_place(shared[i])[0] for i in range(2)]
+    most = jnp.zeros((NZ * NX, 1), jnp.int32)
     for s in range(NX):
-        hits = ((source == s) & (chip != s)).astype(jnp.int32)
-        most = jnp.maximum(most, jnp.max(jnp.sum(hits, axis=1, keepdims=True)))
-    most_ref[0] = most
-
-    @pl.loop(0, NZ * 8)
+        asked = jnp.sum((source == s).astype(jnp.int32), axis=1, keepdims=True)
+        asked += sum((holder == s).astype(jnp.int32) for holder in holders)
+        most = jnp.maximum(most, jnp.where(chip == s, 0, asked))
+    most_ref[0] = jnp.max(most)
+
+    @pl.loop(0, NZ * 8, unroll=8)
     def _(at):
         last_ref[at] = TERMS
 
-    @pl.loop(0, 3 * CAP)
+    @pl.loop(0, 3 * CAP, unroll=5)
     def _(n):
         at_ref[n] = 0
         back_ref[n] = 0
@@ -670,12 +675,24 @@
     for r in range(NX):
         count[r] = 0
 
-    @pl.loop(0, SLOTS)
-    def _(slot):
-        holder, at = block_place(table[(z * NX + x) * SLOTS + slot])
-        pos_ref[slot] = 0
+    def visit_all(chip, visit):
+        row = z * NX + lax.rem(chip, NX)
+
+        @pl.loop(0, REQ, unroll=2)
+        def _(i):
+            visit(i, *block_place(pairs[row, i]))
+
+        for i in range(2):
+            visit(REQ + i, *block_place(shared[i]))
+
+        @pl.loop(0, REQ, unroll=2)
+        def _(i):
+            visit(REQ + 2 + i, *block_place(pairs[row, REQ + i]))
+
+    def request(slot, holder, at):
+        r = lax.rem(holder - x + NX, NX)
+        code_ref[slot] = at
         prev_ref[slot] = TERMS
-        r = lax.rem(holder - x + NX, NX)
 
         @pl.when(r == 0)
         def _():
@@ -689,45 +706,59 @@
 
             @pl.when(j < CAP)
             def _():
-                pos_ref[slot] = (r - 1) * CAP + j
+                code_ref[slot] = NZ * 8 + (r - 1) * CAP + j
                 back_ref[(r - 1) * CAP + j] = slot
 
+    visit_all(x, request)
     for r in range(1, NX):
         count[0] = 0
 
-        @pl.loop(0, SLOTS)
-        def _(slot):
-            holder, at = block_place(table[(z * NX + lax.rem(x + r, NX)) * SLOTS + slot])
-
-            @pl.when(holder == x)
+        def serve(slot, holder, at):
+            j = count[0]
+
+            @pl.when((holder == x) & (j < CAP))
             def _():
-                j = count[0]
+                n = (r - 1) * CAP + j
                 count[0] = j + 1
-
-                @pl.when(j < CAP)
-                def _():
-                    n = (r - 1) * CAP + j
-                    at_ref[n] = at
-                    prev_ref[SLOTS + n] = last_ref[at]
-                    last_ref[at] = SLOTS + n
-
-
-def make_lists(table):
+                at_ref[n] = at
+                prev_ref[SLOTS + n] = last_ref[at]
+                last_ref[at] = SLOTS + n
+
+        visit_all(x + r, serve)
+
+
+def make_lists(pairs, shared):
     smem = pl.BlockSpec(memory_space=pltpu.SMEM)
     vmem = pl.BlockSpec(memory_space=pltpu.VMEM)
     sizes = (3 * CAP, SLOTS, 3 * CAP, TERMS, NZ * 8, 1)
     return pl.pallas_call(
         list_kernel,
         out_shape=tuple(jax.ShapeDtypeStruct((size,), jnp.int32) for size in sizes),
-        in_specs=[smem, vmem],
+        in_specs=[smem, smem, vmem],
         out_specs=(smem,) * 6,
         scratch_shapes=[pltpu.SMEM((NX,), jnp.int32)],
         name="make_lists",
-    )(table.reshape(-1), table)
+    )(pairs, shared, pairs)
+
+
+ORDER = (
+    ("z_start", 0), ("z_start", 1), ("z1", 0), ("z2", 0), ("z3", 0),
+    ("z4", 0), ("z1", 1), ("x_start", 0), ("z2", 1), ("z3", 1),
+    ("z4", 1), ("x_start", 1), ("z_start", 2), ("z_start", 3), ("x_finish", 0),
+    ("attend", 0), ("z1", 3), ("back_x", 0), ("z2", 3), ("z3", 3),
+    ("x_finish", 1), ("z4", 3), ("z1", 2), ("x_start", 3), ("land", 0),
+    ("z2", 2), ("attend", 1), ("back_x", 1), ("b4", 0), ("z3", 2),
+    ("b3", 0), ("x_finish", 3), ("attend", 3), ("z4", 2), ("x_start", 2),
+    ("b2", 0), ("b1", 0), ("land", 1), ("b4", 1), ("back_x", 3),
+    ("finish", 0), ("b3", 1), ("b2", 1), ("x_finish", 2), ("attend", 2),
+    ("back_x", 2), ("b1", 1), ("land", 3), ("b4", 3), ("b3", 3),
+    ("b2", 3), ("land", 2), ("b4", 2), ("b3", 2), ("finish", 1),
+    ("b1", 3), ("b2", 2), ("finish", 3), ("b1", 2), ("finish", 2),
+)
 
 
 def layer_kernel(
-    table, at_list, pos_list, back_list, prev, last, q_ref, g_ref, k_ref, v_ref,
+    at_list, code_list, back_list, prev, last, q_ref, g_ref, k_ref, v_ref,
     att_ref, qg_ref, wacc_ref, out_ref, edge_ref,
     packed, give, kv, halo, wide, window, shared, terms, rim,
     theirs, own, back_packed, arrived, chain, landed, send_buf, recv_buf, give_back,
@@ -816,8 +847,9 @@
             x_copy(p, r).start()
 
     def chosen(p, slot):
-        holder, at = block_place(table[(z * NX + x) * SLOTS + slot])
-        return jnp.where(holder == x, ag[p][at], landing[p][pos_list[slot]])
+        code = code_list[slot]
+        held = ag[p][jnp.minimum(code, NZ * 8 - 1)]
+        return jnp.where(code < NZ * 8, held, landing[p][jnp.maximum(code - NZ * 8, 0)])
 
     def handed(p):
         return remote(give.at[p], kv.at[p, c], give_sem.at[0, p], give_sem.at[1, p], sibling)
@@ -1024,38 +1056,32 @@
                 )
             )
 
-    def turn_of(p, turn):
-        step = turn - 2 * p
-        if step == 0:
-            z_start(p)
-        if 1 <= step <= 4:
-            z_step(p, step)
-        if step == 4:
-            x_start(p)
-        if step == 7:
-            x_finish(p)
-        if step == 8:
-            if p == 0:
-                for copy in halos:
-                    copy.wait()
-            attend_part(p)
-            if p == PARTS - 1:
+    steps = {
+        "z_start": z_start,
+        "x_start": x_start,
+        "x_finish": x_finish,
+        "attend": attend_part,
+        "back_x": bx_start,
+        "land": land,
+        "finish": bz_finish,
+    }
+    for i in range(1, 5):
+        steps[f"z{i}"] = functools.partial(z_step, step=i)
+        steps[f"b{i}"] = functools.partial(bz_step, distance=i)
+    attended = 0
+    for number, (name, p) in enumerate(ORDER):
+        if name == "attend" and not attended:
+            for copy in halos:
+                copy.wait()
+        steps[name](p)
+        if number == 2:
+            for copy in halos:
+                copy.start()
+        if name == "attend":
+            attended += 1
+            if attended == PARTS:
                 for copy in edges:
                     copy.start()
-            bx_start(p)
-        if step == 12:
-            land(p)
-        if 12 <= step <= 15:
-            bz_step(p, 16 - step)
-        if step == 16:
-            bz_finish(p)
-
-    for turn in range(2 * PARTS + 15):
-        for p in range(PARTS):
-            turn_of(p, turn)
-        if turn == 3:
-            for copy in halos:
-                copy.start()
 
     for copy in edges:
         copy.wait()
@@ -1071,7 +1097,7 @@
         handed_back(p).wait()
 
 
-def layer(table, lists, q, g, k, v):
+def layer(lists, q, g, k, v):
     features = k.shape[-1]
     vmem = pl.BlockSpec(memory_space=pltpu.VMEM)
     smem = pl.BlockSpec(memory_space=pltpu.SMEM)
@@ -1091,7 +1117,7 @@
             jax.ShapeDtypeStruct((2, BLK_DEV, BLK, features), bf16),
             jax.ShapeDtypeStruct((2, 2, BLK, features), bf16),
         ),
-        in_specs=[smem] * 6 + [vmem] * 4,
+        in_specs=[smem] * 5 + [vmem] * 4,
         out_specs=(vmem,) * 5,
         scratch_shapes=[
             tiles(PARTS, 3 * CAP), tiles(PARTS, REQ + 2), tiles(PARTS, 2, REQ + 2),
@@ -1112,27 +1138,26 @@
             collective_id=2, has_side_effects=True, vmem_limit_bytes=VMEM_LIMIT
         ),
         name="layer",
-    )(table, *lists, q, g, k, v)
+    )(*lists, q, g, k, v)
 
 
 def per_device(queries, key_rows, value_rows, out_grad, random_blocks, global_blocks):
     row_count, features = queries.shape
     blocks = (BLK_DEV, BLK, features)
-    lists = random_blocks.reshape(NZ * NX, NC, REQ)
-    shared = jnp.broadcast_to(global_blocks[None], (NZ * NX, 2))
-    table = jnp.concatenate([lists[:, 0], shared, lists[:, 1]], axis=1)
     k = key_rows.reshape(blocks)
     v = value_rows.reshape(blocks)
     q = queries.reshape(blocks)
     g = out_grad.reshape(blocks)
-    *packed_lists, most = make_lists(table)
+    *packed_lists, most = make_lists(random_blocks.reshape(NZ * NX, 2 * REQ), global_blocks)
 
     def packed():
-        attended, query_grad, *parts = layer(table.reshape(-1), packed_lists, q, g, k, v)
+        attended, query_grad, *parts = layer(packed_lists, q, g, k, v)
         return attended, query_grad, *joined(*parts)
 
     def unpacked():
-        flat = table.reshape(-1)
+        lists = random_blocks.reshape(NZ * NX, NC, REQ)
+        shared = jnp.broadcast_to(global_blocks[None], (NZ * NX, 2))
+        flat = jnp.concatenate([lists[:, 0], shared, lists[:, 1]], axis=1).reshape(-1)
         prev, last = plan(flat)
         slots, halo = gather(flat, k, v)
         attended, query_grad, wacc, terms, rims = attend(q, g, k, v, halo, slots)

time: 160 us -> 151 us (0.944)
  Pallas kernels: 151 us -> 144 us
    pallas_call x1, Pallas kernels: 147 us -> 141 us  [layer(): pl.pallas_call(layer_kernel, out_shape=(jax.ShapeDtypeStruct((BLK_DEV, BL...]
where the time goes in v6:
time: 151 us; the launch traced here: 150 us
  Pallas kernels  144 us (95%)
  local copies, waits for them, and re-layouts  3.04 us (2%)
  other arithmetic  1.77 us (1%)
    pallas_call x1, Pallas kernels, layer(): pl.pallas_call(layer_kernel, out_shape=(jax.ShapeDtypeStruct((BLK_DEV, BL...  141 us
    pallas_call x1, Pallas kernels, make_lists(): pl.pallas_call(list_kernel, out_shape=tuple((jax.ShapeDtypeStruct((size,)...  3.57 us

profile of v6, /device:TPU:1, one launch (start us, length us, event | category | flops | bytes accessed | tf_op | source)
XLA Modules:
  0.0 150.5 jit_solution(13828793228648135075)
XLA Ops:
  0.6 0.8 copy.13
  1.5 0.7 reshape.194.pairs.wide_ref
  2.2 3.6 %make_lists.1 = (s32[45]{0:T(128)S(1)}, s32[26]{0:T(128)S(1)}, s32[45]{0:T(128)S(1)}, s32[71]{0:T(128)S(1)}, s32[64]{0:T(128)S(1)}, /*index=5*/s32[1]{0:T(128)}) custom-call(s32[32,24]{1,0:T(8,128)} %reshape.194.pairs.wide_ref, s32[2]{0:T(128)} %shared.1, s32[32,24]{1,0:T(8,128)} %reshape.194.pairs.wide_ref), custom_call_target="tpu_custom_call" | custom-call | tf_op jit(solution)/shard_map/make_lists/pallas_call | solution.py:734
  6.4 142.6 %conditional.1 = (bf16[4,64,512]{2,1,0:T(8,128)(2,1)S(1)}, bf16[4,64,512]{2,1,0:T(8,128)(2,1)S(1)}, bf16[256,512]{1,0:T(8,128)(2,1)S(1)}, bf16[256,512]{1,0:T(8,128)(2,1)S(1)}) conditional(s32[]{:T(128)} %bitcast.6, (s32[1,256,3]{1,0,2:T(1,128)}, s32[2]{0:T(128)}, bf16[4,64,512]{2,1,0:T(8,128)(2,1)}, bf16[4,64,512]{2,1,0:T(8,128)(2,1)}, ...), branch_computations={%region_0.1_spmd, %region_1.2_spmd} | conditional | flops 1050240 | bytes 11828276 | solution.py:1167
  6.4 140.5 %layer.1 = (bf16[4,64,512]{2,1,0:T(8,128)(2,1)S(1)}, bf16[4,64,512]{2,1,0:T(8,128)(2,1)S(1)}, f32[2,4,64,512]{3,2,1,0:T(8,128)}, bf16[2,4,64,512]{3,2,1,0:T(8,128)(2,1)}, bf16[2,2,64,512]{3,2,1,0:T(8,128)(2,1)}) custom-call(s32[45]{0:T(128)S(1)} %get-tuple-element.97.at_list, s32[26]{0:T(128)S(1)} %get-tuple-element.98.code_list, ...), custom_call_target="tpu_custom_call" | custom-call | tf_op jit(solution)/shard_map/cond/branch_1_fun/layer/pallas_call | solution.py:1111
  146.9 0.0 copy-start.2
  146.9 1.6 %convert_add_fusion.1 = f32[2,4,64,512]{3,2,1,0:T(8,128)S(1)} fusion(f32[2,4,64,512]{3,2,1,0:T(8,128)} %get-tuple-element.108, bf16[2,4,64,512]{3,2,1,0:T(8,128)(2,1)} %get-tuple-element.109), kind=kLoop, calls=%fused_computation.6 | loop fusion | flops 524288 | bytes 2621440 | tf_op jit(solution)/shard_map/cond/branch_1_fun/add | solution.py:1172
  148.5 0.0 copy-done.2
  148.5 0.1 fusion.3
  148.6 0.1 fusion.2
  148.7 0.1 convert_element_type.31
  149.0 0.0 copy-start.3
  149.0 0.0 copy-start.4
  149.0 0.8 copy.30
  149.8 0.7 copy.31
  150.5 0.0 copy-done.3
  150.5 0.0 copy-done.4
  (1 shorter events, 0.0 us)
Async XLA Ops:
  146.9 1.6 %copy-start.2 = (bf16[2,2,64,512]{3,2,1,0:T(8,128)(2,1)S(1)}, bf16[2,2,64,512]{3,2,1,0:T(8,128)(2,1)}, u32[]{:S(2)}) copy-start(bf16[2,2,64,512]{3,2,1,0:T(8,128)(2,1)} %get-tuple-element.110) | copy-start | bytes 786436 | tf_op jit(solution)/shard_map/cond
  149.0 1.5 copy-start.3
  149.0 1.5 copy-start.4

commit v7 on v6

--- a/solution.py
+++ b/solution.py
@@ -742,18 +742,18 @@
 
 
 ORDER = (
-    ("z_start", 0), ("z_start", 1), ("z1", 0), ("z2", 0), ("z3", 0),
-    ("z4", 0), ("z1", 1), ("x_start", 0), ("z2", 1), ("z3", 1),
-    ("z4", 1), ("x_start", 1), ("z_start", 2), ("z_start", 3), ("x_finish", 0),
-    ("attend", 0), ("z1", 3), ("back_x", 0), ("z2", 3), ("z3", 3),
-    ("x_finish", 1), ("z4", 3), ("z1", 2), ("x_start", 3), ("land", 0),
-    ("z2", 2), ("attend", 1), ("back_x", 1), ("b4", 0), ("z3", 2),
-    ("b3", 0), ("x_finish", 3), ("attend", 3), ("z4", 2), ("x_start", 2),
-    ("b2", 0), ("b1", 0), ("land", 1), ("b4", 1), ("back_x", 3),
-    ("finish", 0), ("b3", 1), ("b2", 1), ("x_finish", 2), ("attend", 2),
-    ("back_x", 2), ("b1", 1), ("land", 3), ("b4", 3), ("b3", 3),
-    ("b2", 3), ("land", 2), ("b4", 2), ("b3", 2), ("finish", 1),
-    ("b1", 3), ("b2", 2), ("finish", 3), ("b1", 2), ("finish", 2),
+    ("z_start", 0), ("z_start", 1), ("z1", 0), ("z2", 0), ("z1", 1),
+    ("z3", 0), ("z4", 0), ("x_start", 0), ("z2", 1), ("z_start", 2),
+    ("z3", 1), ("z1", 2), ("z4", 1), ("z_start", 3), ("x_start", 1),
+    ("x_finish", 0), ("attend", 0), ("z2", 2), ("back_x", 0), ("z1", 3),
+    ("z3", 2), ("z2", 3), ("z4", 2), ("x_start", 2), ("x_finish", 1),
+    ("z3", 3), ("land", 0), ("attend", 1), ("z4", 3), ("back_x", 1),
+    ("b4", 0), ("x_start", 3), ("x_finish", 2), ("attend", 2), ("back_x", 2),
+    ("b3", 0), ("land", 1), ("b4", 1), ("b2", 0), ("b3", 1),
+    ("b2", 1), ("x_finish", 3), ("b1", 0), ("attend", 3), ("b1", 1),
+    ("back_x", 3), ("land", 2), ("finish", 0), ("b4", 2), ("b3", 2),
+    ("b2", 2), ("land", 3), ("b4", 3), ("b1", 2), ("b3", 3),
+    ("b2", 3), ("finish", 2), ("finish", 1), ("b1", 3), ("finish", 3),
 )
 
 

time: 151 us -> 152 us (level)
  no operation moved by 1% of the time
where the time goes in v7:
time: 152 us; the launch traced here: 151 us
  Pallas kernels  145 us (95%)
  local copies, waits for them, and re-layouts  3.04 us (2%)
  other arithmetic  1.77 us (1%)
    pallas_call x1, Pallas kernels, layer(): pl.pallas_call(layer_kernel, out_shape=(jax.ShapeDtypeStruct((BLK_DEV, BL...  141 us
    pallas_call x1, Pallas kernels, make_lists(): pl.pallas_call(list_kernel, out_shape=tuple((jax.ShapeDtypeStruct((size,)...  3.57 us

profile of v7, /device:TPU:1, one launch (start us, length us, event | category | flops | bytes accessed | tf_op | source)
XLA Modules:
  0.0 151.3 jit_solution(16706302859165807954)
XLA Ops:
  0.6 0.8 copy.13
  1.5 0.7 reshape.194.pairs.wide_ref
  2.2 3.6 %make_lists.1 = (s32[45]{0:T(128)S(1)}, s32[26]{0:T(128)S(1)}, s32[45]{0:T(128)S(1)}, s32[71]{0:T(128)S(1)}, s32[64]{0:T(128)S(1)}, /*index=5*/s32[1]{0:T(128)}) custom-call(s32[32,24]{1,0:T(8,128)} %reshape.194.pairs.wide_ref, s32[2]{0:T(128)} %shared.1, s32[32,24]{1,0:T(8,128)} %reshape.194.pairs.wide_ref), custom_call_target="tpu_custom_call" | custom-call | tf_op jit(solution)/shard_map/make_lists/pallas_call | solution.py:734
  6.4 143.4 %conditional.1 = (bf16[4,64,512]{2,1,0:T(8,128)(2,1)S(1)}, bf16[4,64,512]{2,1,0:T(8,128)(2,1)S(1)}, bf16[256,512]{1,0:T(8,128)(2,1)S(1)}, bf16[256,512]{1,0:T(8,128)(2,1)S(1)}) conditional(s32[]{:T(128)} %bitcast.6, (s32[1,256,3]{1,0,2:T(1,128)}, s32[2]{0:T(128)}, bf16[4,64,512]{2,1,0:T(8,128)(2,1)}, bf16[4,64,512]{2,1,0:T(8,128)(2,1)}, ...), branch_computations={%region_0.1_spmd, %region_1.2_spmd} | conditional | flops 1050240 | bytes 11828276 | solution.py:1167
  6.4 141.3 %layer.1 = (bf16[4,64,512]{2,1,0:T(8,128)(2,1)S(1)}, bf16[4,64,512]{2,1,0:T(8,128)(2,1)S(1)}, f32[2,4,64,512]{3,2,1,0:T(8,128)}, bf16[2,4,64,512]{3,2,1,0:T(8,128)(2,1)}, bf16[2,2,64,512]{3,2,1,0:T(8,128)(2,1)}) custom-call(s32[45]{0:T(128)S(1)} %get-tuple-element.97.at_list, s32[26]{0:T(128)S(1)} %get-tuple-element.98.code_list, ...), custom_call_target="tpu_custom_call" | custom-call | tf_op jit(solution)/shard_map/cond/branch_1_fun/layer/pallas_call | solution.py:1111
  147.7 0.0 copy-start.2
  147.7 1.6 %convert_add_fusion.1 = f32[2,4,64,512]{3,2,1,0:T(8,128)S(1)} fusion(f32[2,4,64,512]{3,2,1,0:T(8,128)} %get-tuple-element.108, bf16[2,4,64,512]{3,2,1,0:T(8,128)(2,1)} %get-tuple-element.109), kind=kLoop, calls=%fused_computation.6 | loop fusion | flops 524288 | bytes 2621440 | tf_op jit(solution)/shard_map/cond/branch_1_fun/add | solution.py:1172
  149.3 0.0 copy-done.2
  149.3 0.1 fusion.3
  149.4 0.1 fusion.2
  149.5 0.1 convert_element_type.31
  149.8 0.0 copy-start.3
  149.8 0.0 copy-start.4
  149.9 0.8 copy.30
  150.6 0.7 copy.31
  151.3 0.0 copy-done.3
  151.3 0.0 copy-done.4
  (1 shorter events, 0.0 us)
Async XLA Ops:
  147.7 1.6 %copy-start.2 = (bf16[2,2,64,512]{3,2,1,0:T(8,128)(2,1)S(1)}, bf16[2,2,64,512]{3,2,1,0:T(8,128)(2,1)}, u32[]{:S(2)}) copy-start(bf16[2,2,64,512]{3,2,1,0:T(8,128)(2,1)} %get-tuple-element.110) | copy-start | bytes 786436 | tf_op jit(solution)/shard_map/cond
  149.8 1.5 copy-start.3
  149.8 1.5 copy-start.4

commit v8 on v6

--- a/solution.py
+++ b/solution.py
@@ -666,6 +666,8 @@
     def _(at):
         last_ref[at] = TERMS
 
+    last_ref[NZ * 8] = TERMS
+
     @pl.loop(0, 3 * CAP, unroll=5)
     def _(n):
         at_ref[n] = 0
@@ -678,36 +680,28 @@
     def visit_all(chip, visit):
         row = z * NX + lax.rem(chip, NX)
 
-        @pl.loop(0, REQ, unroll=2)
+        @pl.loop(0, REQ, unroll=4)
         def _(i):
             visit(i, *block_place(pairs[row, i]))
 
         for i in range(2):
             visit(REQ + i, *block_place(shared[i]))
 
-        @pl.loop(0, REQ, unroll=2)
+        @pl.loop(0, REQ, unroll=4)
         def _(i):
             visit(REQ + 2 + i, *block_place(pairs[row, REQ + i]))
 
     def request(slot, holder, at):
         r = lax.rem(holder - x + NX, NX)
-        code_ref[slot] = at
-        prev_ref[slot] = TERMS
-
-        @pl.when(r == 0)
-        def _():
-            prev_ref[slot] = last_ref[at]
-            last_ref[at] = slot
-
-        @pl.when(r > 0)
-        def _():
-            j = count[r]
-            count[r] = j + 1
-
-            @pl.when(j < CAP)
-            def _():
-                code_ref[slot] = NZ * 8 + (r - 1) * CAP + j
-                back_ref[(r - 1) * CAP + j] = slot
+        j = count[r]
+        count[r] = j + 1
+        fits = (r > 0) & (j < CAP)
+        n = jnp.where(fits, (r - 1) * CAP + j, 3 * CAP)
+        code_ref[slot] = jnp.where(fits, NZ * 8 + n, at)
+        back_ref[n] = slot
+        chained = jnp.where(r == 0, at, NZ * 8)
+        prev_ref[slot] = jnp.where(r == 0, last_ref[chained], TERMS)
+        last_ref[chained] = slot
 
     visit_all(x, request)
     for r in range(1, NX):
@@ -715,14 +709,13 @@
 
         def serve(slot, holder, at):
             j = count[0]
-
-            @pl.when((holder == x) & (j < CAP))
-            def _():
-                n = (r - 1) * CAP + j
-                count[0] = j + 1
-                at_ref[n] = at
-                prev_ref[SLOTS + n] = last_ref[at]
-                last_ref[at] = SLOTS + n
+            hit = (holder == x) & (j < CAP)
+            count[0] = j + hit.astype(jnp.int32)
+            n = jnp.where(hit, (r - 1) * CAP + j, 3 * CAP)
+            at_ref[n] = at
+            chained = jnp.where(hit, at, NZ * 8)
+            prev_ref[SLOTS + n] = last_ref[chained]
+            last_ref[chained] = SLOTS + n
 
         visit_all(x + r, serve)
 
@@ -730,7 +723,7 @@
 def make_lists(pairs, shared):
     smem = pl.BlockSpec(memory_space=pltpu.SMEM)
     vmem = pl.BlockSpec(memory_space=pltpu.VMEM)
-    sizes = (3 * CAP, SLOTS, 3 * CAP, TERMS, NZ * 8, 1)
+    sizes = (3 * CAP + 1, SLOTS, 3 * CAP + 1, TERMS + 1, NZ * 8 + 1, 1)
     return pl.pallas_call(
         list_kernel,
         out_shape=tuple(jax.ShapeDtypeStruct((size,), jnp.int32) for size in sizes),
@@ -838,7 +831,7 @@
         )
 
     def x_start(p):
-        for r in (2, 1, 3):
+        for r in (1, 3, 2):
             @pl.loop(0, CAP, unroll=3)
             def _(j):
                 n = (r - 1) * CAP + j
@@ -971,7 +964,7 @@
                 jnp.float32
             )
             own[p, REQ + i] = total.astype(jnp.bfloat16)
-        for r in (2, 1, 3):
+        for r in (1, 3, 2):
             @pl.loop(0, CAP, unroll=3)
             def _(j):
                 n = (r - 1) * CAP + j

time: 151 us -> 151 us (level)
  no operation moved by 1% of the time
where the time goes in v8:
time: 151 us
  Pallas kernels  145 us (96%)
  local copies, waits for them, and re-layouts  3.04 us (2%)
  other arithmetic  1.77 us (1%)
    pallas_call x1, Pallas kernels, layer(): pl.pallas_call(layer_kernel, out_shape=(jax.ShapeDtypeStruct((BLK_DEV, BL...  141 us
    pallas_call x1, Pallas kernels, make_lists(): pl.pallas_call(list_kernel, out_shape=tuple((jax.ShapeDtypeStruct((size,)...  3.41 us

profile of v8, /device:TPU:1, one launch (start us, length us, event | category | flops | bytes accessed | tf_op | source)
XLA Modules:
  0.0 151.0 jit_solution(8528344483350158842)
XLA Ops:
  0.6 0.8 copy.13
  1.5 0.7 reshape.194.pairs.wide_ref
  2.2 3.4 %make_lists.1 = (s32[46]{0:T(128)S(1)}, s32[26]{0:T(128)S(1)}, s32[46]{0:T(128)S(1)}, s32[72]{0:T(128)S(1)}, s32[65]{0:T(128)S(1)}, /*index=5*/s32[1]{0:T(128)}) custom-call(s32[32,24]{1,0:T(8,128)} %reshape.194.pairs.wide_ref, s32[2]{0:T(128)} %shared.1, s32[32,24]{1,0:T(8,128)} %reshape.194.pairs.wide_ref), custom_call_target="tpu_custom_call" | custom-call | tf_op jit(solution)/shard_map/make_lists/pallas_call | solution.py:727
  6.2 143.3 %conditional.1 = (bf16[4,64,512]{2,1,0:T(8,128)(2,1)S(1)}, bf16[4,64,512]{2,1,0:T(8,128)(2,1)S(1)}, bf16[256,512]{1,0:T(8,128)(2,1)S(1)}, bf16[256,512]{1,0:T(8,128)(2,1)S(1)}) conditional(s32[]{:T(128)} %bitcast.6, (s32[1,256,3]{1,0,2:T(1,128)}, s32[2]{0:T(128)}, bf16[4,64,512]{2,1,0:T(8,128)(2,1)}, bf16[4,64,512]{2,1,0:T(8,128)(2,1)}, ...), branch_computations={%region_0.1_spmd, %region_1.2_spmd} | conditional | flops 1050240 | bytes 11828276 | solution.py:1160
  6.2 141.1 %layer.1 = (bf16[4,64,512]{2,1,0:T(8,128)(2,1)S(1)}, bf16[4,64,512]{2,1,0:T(8,128)(2,1)S(1)}, f32[2,4,64,512]{3,2,1,0:T(8,128)}, bf16[2,4,64,512]{3,2,1,0:T(8,128)(2,1)}, bf16[2,2,64,512]{3,2,1,0:T(8,128)(2,1)}) custom-call(s32[46]{0:T(128)S(1)} %get-tuple-element.97.at_list, s32[26]{0:T(128)S(1)} %get-tuple-element.98.code_list, ...), custom_call_target="tpu_custom_call" | custom-call | tf_op jit(solution)/shard_map/cond/branch_1_fun/layer/pallas_call | solution.py:1104
  147.4 0.0 copy-start.2
  147.4 1.6 %convert_add_fusion.1 = f32[2,4,64,512]{3,2,1,0:T(8,128)S(1)} fusion(f32[2,4,64,512]{3,2,1,0:T(8,128)} %get-tuple-element.108, bf16[2,4,64,512]{3,2,1,0:T(8,128)(2,1)} %get-tuple-element.109), kind=kLoop, calls=%fused_computation.6 | loop fusion | flops 524288 | bytes 2621440 | tf_op jit(solution)/shard_map/cond/branch_1_fun/add | solution.py:1165
  149.0 0.0 copy-done.2
  149.0 0.1 fusion.3
  149.1 0.1 fusion.2
  149.1 0.1 convert_element_type.31
  149.5 0.0 copy-start.3
  149.5 0.0 copy-start.4
  149.5 0.8 copy.30
  150.3 0.7 copy.31
  151.0 0.0 copy-done.3
  151.0 0.0 copy-done.4
  (1 shorter events, 0.0 us)
Async XLA Ops:
  147.4 1.6 %copy-start.2 = (bf16[2,2,64,512]{3,2,1,0:T(8,128)(2,1)S(1)}, bf16[2,2,64,512]{3,2,1,0:T(8,128)(2,1)}, u32[]{:S(2)}) copy-start(bf16[2,2,64,512]{3,2,1,0:T(8,128)(2,1)} %get-tuple-element.110) | copy-start | bytes 786436 | tf_op jit(solution)/shard_map/cond
  149.5 1.5 copy-start.3
  149.5 1.5 copy-start.4
